TPU v7x, 32 devices: a whole 2x2x4 slice. The times are simulated.
32 devices in a mesh: ctx: 8 (over z, x), tp: 4 (over y, core).
Axes of the slice: x: 2, y: 2, z: 4, core: 2. Of those that a mesh axis runs over, the one named last changes fastest.
Arguments:
- queries: bfloat16 [2048, 1024], P('ctx', 'tp'), may hold values from -6 to 6
- keys: bfloat16 [2048, 1024], P('ctx', 'tp'), may hold values from -6 to 6
- values: bfloat16 [2048, 1024], P('ctx', 'tp'), may hold values from -20 to 20, as said below
- gain: float32 [1024], P('tp'), may hold values from 0.25 to 1.75
- out_grad: bfloat16 [2048, 1024], P('ctx', 'tp'), may hold values from -6 to 6
Outputs:
- normed: bfloat16 [2048, 1024], P('ctx', 'tp')
- grad_queries: bfloat16 [2048, 1024], P('ctx', 'tp')
- grad_keys: bfloat16 [2048, 1024], P('ctx', 'tp')
- grad_values: bfloat16 [2048, 1024], P('ctx', 'tp')
Inputs may be any that keep to these rules, and one draw needn't show every extreme that they name: values of order one, each head at its own scale.
All inputs are finite; a program needn't handle non-finite values.
Results may differ from a plain program's by a relative error of at most 0.0065.
Values sent between devices are 32-bit elements; how exact they have to be, the bound alone decides.
No kernel may reach another device: no remote copies, remote signals or barrier semaphores. Data moves between devices by JAX's collectives and lax.ppermute only.
A program may use at most 64 MiB of HBM per device.

v0:
```python
import functools

import jax
import jax.numpy as jnp
from jax import lax
from jax.experimental import pallas as pl
from jax.experimental.pallas import tpu as pltpu
from jax.sharding import PartitionSpec as P

HEAD = 128

epsilon = 1e-06
LOADS = 4
FIRST, BACK, HAND = 0, 1, 2
ALONE = (0, 2)
SHARED = (1, 3)
F32 = jnp.float32
BF16 = jnp.bfloat16

NN = (((1,), (0,)), ((), ()))
NT = (((1,), (1,)), ((), ()))
TN = (((0,), (0,)), ((), ()))


def dot(a, b, dims):
    return lax.dot_general(a, b, dims, preferred_element_type=F32)


VMEM = pl.BlockSpec(memory_space=pltpu.VMEM)
HBM = pl.BlockSpec(memory_space=pltpu.HBM)


def call(body, outs, *args, ins=None, dests=None, scratch=(), flops=1e7):
    moved = sum(a.size * a.dtype.itemsize for a in args)
    return pl.pallas_call(
        body,
        out_shape=outs,
        in_specs=ins or [VMEM] * len(args),
        out_specs=dests or jax.tree.map(lambda _: VMEM, outs),
        scratch_shapes=scratch,
        compiler_params=pltpu.CompilerParams(vmem_limit_bytes=16 * 1024 * 1024),
        cost_estimate=pl.CostEstimate(flops=int(flops), bytes_accessed=int(moved), transcendentals=0),
    )(*args)


def head(h):
    return slice(h * HEAD, (h + 1) * HEAD)


def causal_mask(tokens):
    row = lax.broadcasted_iota(jnp.int32, (tokens, tokens), 0)
    col = lax.broadcasted_iota(jnp.int32, (tokens, tokens), 1)
    return row >= col


def rows_of(scratch, parts, place):
    rows = scratch.shape[0] // parts
    return scratch.at[pl.ds(pl.multiple_of(place * rows, rows), rows), :]


def step_of(i, odd, order):
    return (
        (3, 2, 1, 0),
        (3, 2, 1, 0),
        (3 - 2 * odd, 2 + odd, 1 + odd, 0),
    )[order][i]


def give(scratch, group, outs, order=0):
    if len(outs) == 1:
        outs[0][...] = scratch[...].reshape(outs[0].shape)
        return
    place = lax.rem(lax.axis_index("ctx"), group)
    odd = lax.rem(lax.axis_index("tp"), 2)
    for i, out in enumerate(outs):
        out[...] = rows_of(scratch, group, lax.bitwise_xor(place, step_of(i, odd, order)))[...]


def take(ins, scratch, group, order=0):
    if len(ins) == 1:
        scratch[...] = ins[0][...].reshape(scratch.shape)
        return
    place = lax.rem(lax.axis_index("ctx"), group)
    sent_by_odd = 1 - lax.rem(lax.axis_index("tp"), 2)
    for i, piece in enumerate(ins):
        rows_of(scratch, group, lax.bitwise_xor(place, step_of(i, sent_by_odd, order)))[...] = piece[...]


def running_sums(scratch, parts, reverse):
    rows = scratch.shape[0] // parts
    running = jnp.zeros((rows, scratch.shape[1]), F32)
    for place in range(parts - 1, -1, -1) if reverse else range(parts):
        own = slice(place * rows, (place + 1) * rows)
        here = scratch[own, :]
        scratch[own, :] = running
        running = running + here
    return running


def loads(pairs, sems):
    copies = [pltpu.make_async_copy(a, b, sems.at[i]) for i, (a, b) in enumerate(pairs)]
    for copy in copies:
        copy.start()
    return copies


def states_body(heads, group, k_hbm, v_hbm, k, v, *refs):
    outs, (state, sems) = refs[:-2], refs[-2:]
    rows = k.shape[0] // LOADS
    blocks = [slice(i * rows, (i + 1) * rows) for i in range(LOADS)]
    for copy in loads([(a.at[r, :], b.at[r, :]) for r in blocks for a, b in ((k_hbm, k), (v_hbm, v))], sems):
        copy.wait()
    for h in range(heads):
        state[head(h), :] = dot(k[:, head(h)], v[:, head(h)], TN)
    give(state, group, outs[:group], FIRST)
    for again, i in zip(outs[group:], ALONE):
        again[...] = outs[i][...]


def scan_body(count, reverse, arrived, sums, scratch):
    take([arrived], scratch, count)
    running_sums(scratch, count, reverse)
    give(scratch, count, [sums])


def inner_body(group, reverse, *refs):
    arrived, total, outs, sums = refs[:group], refs[group], refs[group + 1 : 2 * group + 1], refs[-1]
    take(arrived, sums, group, BACK if reverse else FIRST)
    total[...] = running_sums(sums, group, reverse)
    give(sums, group, outs, HAND)
    if not reverse:
        for passed, i in zip(refs[2 * group + 1 : -1], SHARED):
            passed[...] = arrived[i][...]


def add_body(group, sums, over, *outs):
    place = lax.rem(lax.axis_index("ctx"), group)
    odd = lax.rem(lax.axis_index("tp"), 2)
    for i, out in enumerate(outs):
        out[...] = rows_of(sums, group, lax.bitwise_xor(place, step_of(i, odd, HAND)))[...] + over[...]


def late_body(group, reverse, *refs):
    arrived, over, outs, sums = refs[:group], refs[group], refs[group + 1 : -1], refs[-1]
    take(arrived, sums, group)
    running_sums(sums, group, reverse)
    add_body(group, sums, over, *outs)


def pick(pieces, scratch, group):
    many = len(pieces) // 2
    if many == 0:
        take(pieces, scratch, group)
        return
    early = lax.axis_index("ctx") < group
    place = lax.rem(lax.axis_index("ctx"), group)
    sent_by_odd = 1 - lax.rem(lax.axis_index("tp"), 2)
    for i in range(many):
        rows = rows_of(scratch, group, lax.bitwise_xor(place, step_of(i, sent_by_odd, HAND)))
        rows[...] = jnp.where(early, pieces[i][...], pieces[many + i][...])


def scores_body(heads, factor, k, v, q_hbm, og_hbm, gain_hbm, scores, attended, q, q_turned, weighted, gain, og, sems):
    copies = loads(((q_hbm, q), (og_hbm, og), (gain_hbm, gain)), sems)
    copies[0].wait()
    q_turned[...] = q[...].T
    causal = causal_mask(q.shape[0])
    for h in range(heads):
        raw = dot(q[:, head(h)], k[:, head(h)], NT) * factor
        sc = jnp.where(causal, raw, 0.0).astype(BF16)
        scores[h] = sc
        attended[:, head(h)] = dot(sc, v[:, head(h)], NN)
    for copy in copies[1:]:
        copy.wait()
    for h in range(heads):
        weighted[:, head(h)] = og[:, head(h)].astype(F32) * gain[h : h + 1, :]


def attend_body(heads, factor, group, q, weighted, local, *refs):
    pieces, (attended, stats, prefix) = refs[:-3], refs[-3:]
    pick(pieces, prefix, group)
    power = 0.0
    inner = 0.0
    for h in range(heads):
        att = factor * dot(q[:, head(h)], prefix[head(h), :].astype(BF16), NN) + local[:, head(h)]
        attended[:, head(h)] = att
        power = power + att * att
        inner = inner + weighted[:, head(h)] * att
    stats[0:1, :] = jnp.sum(power.T, axis=0, keepdims=True)
    stats[1:2, :] = jnp.sum(inner.T, axis=0, keepdims=True)


def grad_body(heads, features, group, ways, attended, weighted, q_turned, *refs):
    stats, (spread, grad), outs, updates = refs[:ways], refs[ways : ways + 2], refs[ways + 2 : -1], refs[-1]
    total = stats[0][...]
    for other in stats[1:]:
        total = total + other[...]
    inv_rms = lax.rsqrt(total[0:1, :] / features + epsilon)
    bend = inv_rms * inv_rms * (total[1:2, :] / features)
    tokens = q_turned.shape[1]
    inv_rms = jnp.broadcast_to(inv_rms, (HEAD, tokens)).T
    bend = jnp.broadcast_to(bend, (HEAD, tokens)).T
    spread[...] = inv_rms
    for h in range(heads):
        ga = (inv_rms * (weighted[:, head(h)] - attended[:, head(h)] * bend)).astype(BF16)
        grad[:, head(h)] = ga
        updates[head(h), :] = dot(q_turned[head(h), :], ga, NN)
    give(updates, group, outs, BACK)


def local_body(heads, factor, ga, q, k, v, prefix, scores, attended, inv_rms, gain, normed, gq, gk_part, gv_part):
    causal = causal_mask(q.shape[0])
    for h in range(heads):
        normed[:, head(h)] = (attended[:, head(h)] * inv_rms[...] * gain[h : h + 1, :]).astype(BF16)
        gah = ga[:, head(h)]
        raw = dot(gah, v[:, head(h)], NT) * factor
        gs = jnp.where(causal, raw, 0.0).astype(BF16)
        out = factor * dot(gah, prefix[head(h), :].astype(BF16), NT)
        gq[:, head(h)] = (out + dot(gs, k[:, head(h)], NN)).astype(BF16)
        gk_part[:, head(h)] = dot(gs, q[:, head(h)], TN)
        gv_part[:, head(h)] = dot(scores[h], gah, TN)


def final_body(heads, factor, group, k, v, gk_part, gv_part, *refs):
    pieces, outs, (suffix, gk, gv, sems) = refs[:-6], refs[-6:-4], refs[-4:]
    pick(pieces, suffix, group)
    copies = []

    def send(h, held, out):
        copy = pltpu.make_async_copy(held.at[:, head(h)], out.at[:, head(h)], sems.at[len(copies)])
        copy.start()
        copies.append(copy)

    for h in range(heads):
        suf = suffix[head(h), :].astype(BF16)
        gk[:, head(h)] = (factor * dot(v[:, head(h)], suf, NT) + gk_part[:, head(h)]).astype(BF16)
        send(h, gk, outs[0])
        gv[:, head(h)] = (factor * dot(k[:, head(h)], suf, NN) + gv_part[:, head(h)]).astype(BF16)
        send(h, gv, outs[1])
    for copy in copies:
        copy.wait()


def exchange(piece, i, active, order):
    ways = lax.axis_size("tp")
    pairs = [
        (j * ways + t, (j ^ step_of(i, t % 2, order) if j in active else j) * ways + (t ^ 1))
        for j in range(lax.axis_size("ctx"))
        for t in range(ways)
    ]
    return lax.ppermute(piece, ("ctx", "tp"), pairs)


def carried_in(pieces, reverse, state):
    again = () if reverse or len(pieces) == 1 else pieces[-len(ALONE) :]
    group = len(pieces) - len(again)
    pieces = pieces[:group]
    count = lax.axis_size("ctx")
    sds = jax.ShapeDtypeStruct
    if group == 1:
        arrived = lax.all_to_all(pieces[0], "ctx", 0, 0, tiled=True)
        sums = call(
            functools.partial(scan_body, count, reverse),
            sds(arrived.shape, F32), arrived, scratch=[state],
        )
        return [lax.all_to_all(sums, "ctx", 0, 0, tiled=True)]
    rows, width = pieces[0].shape
    piece = sds((rows, width), F32)
    early, late, both = range(group), range(group, count), range(count)
    first, second = (late, early) if reverse else (early, late)
    everyone = range(group)
    arrived = [
        exchange(pieces[i], i, both if reverse or i in SHARED else first, BACK if reverse else FIRST)
        for i in everyone
    ]
    kept = [sds((group * rows, width), F32)] if reverse else [piece] * len(SHARED)
    total, *back = call(
        functools.partial(inner_body, group, reverse),
        [piece] * (group + 1) + kept,
        *arrived,
        scratch=[] if reverse else [state],
    )
    over = lax.ppermute(total, "ctx", [(j, j ^ group) for j in both])
    ahead = [exchange(back[i], i, first, HAND) for i in everyone]
    if reverse:
        back = call(functools.partial(add_body, group), [piece] * group, back[group], over)
    else:
        own = [exchange(part, i, second, FIRST) for part, i in zip(again, ALONE)]
        mixed = [own[ALONE.index(i)] if i in ALONE else back[group + SHARED.index(i)] for i in everyone]
        back = call(
            functools.partial(late_body, group, reverse),
            [piece] * group, *mixed, over, scratch=[state],
        )
    behind = [exchange(back[i], i, second, HAND) for i in everyone]
    return [*behind, *ahead] if reverse else [*ahead, *behind]


def from_all(part, axis):
    count = lax.axis_size(axis)
    even = count & (count - 1) == 0
    steps = [1, 3, 2] if count == 4 else range(1, count)
    return [part] + [
        lax.ppermute(part, axis, [(i, i ^ step if even else (i + step) % count) for i in range(count)])
        for step in steps
    ]


def on_device(queries, keys, values, gain, out_grad):
    tokens, width = queries.shape
    heads = width // HEAD
    count = lax.axis_size("ctx")
    factor = (HEAD * tokens * count) ** (-0.5)
    features = width * lax.axis_size("tp")
    gains = gain.reshape(heads, HEAD)
    sds = jax.ShapeDtypeStruct
    wide = sds((tokens, width), F32)
    half = sds((tokens, width), BF16)
    state = pltpu.VMEM((width, HEAD), F32)
    if count == 8 and lax.axis_size("tp") % 2 == 0:
        group = count // 2
        pieces = [sds((width // group, HEAD), F32)] * group
    else:
        group = count
        pieces = [sds((count, width // count, HEAD), F32)]

    def in_hbm(*arrays):
        return [pltpu.with_memory_space_constraint(array, pltpu.HBM) for array in arrays]

    def in_vmem(array):
        return pltpu.VMEM(array.shape, array.dtype)

    k_held, v_held, *states = call(
        functools.partial(states_body, heads, group),
        (in_vmem(keys), in_vmem(values), *pieces, *(pieces[i] for i in ALONE if len(pieces) > 1)),
        *in_hbm(keys, values),
        ins=[HBM, HBM],
        scratch=[state, pltpu.SemaphoreType.DMA((2 * LOADS,))],
    )
    prefix = carried_in(states, False, state)
    pairs = heads * tokens * tokens * HEAD
    scores, local, q_held, q_turned, weighted, gain_held = call(
        functools.partial(scores_body, heads, factor),
        (
            sds((heads, tokens, tokens), BF16), wide,
            in_vmem(queries), pltpu.VMEM((width, tokens), BF16), in_vmem(wide), in_vmem(gains),
        ),
        k_held, v_held, *in_hbm(queries, out_grad, gains),
        ins=[VMEM, VMEM, HBM, HBM, HBM],
        scratch=[in_vmem(out_grad), pltpu.SemaphoreType.DMA((3,))],
        flops=4 * pairs,
    )
    attended, stats, prefix = call(
        functools.partial(attend_body, heads, factor, group),
        (wide, sds((2, tokens), F32), sds((width, HEAD), F32)),
        q_held, weighted, local, *prefix,
    )
    every = from_all(stats, "tp")
    inv_rms, grad_attn, *updates = call(
        functools.partial(grad_body, heads, features, group, len(every)),
        (pltpu.VMEM((tokens, HEAD), F32), half, *pieces),
        attended, weighted, q_turned, *every,
        scratch=[state],
    )
    suffix = carried_in(updates, True, state)
    normed, grad_q, gk_part, gv_part = call(
        functools.partial(local_body, heads, factor),
        (half, half, wide, wide),
        grad_attn, q_held, k_held, v_held, prefix, scores, attended, inv_rms, gain_held,
        flops=9 * pairs,
    )
    held = pltpu.VMEM((tokens, width), BF16)
    grad_k, grad_v = call(
        functools.partial(final_body, heads, factor, group),
        (half, half),
        k_held, v_held, gk_part, gv_part, *suffix,
        dests=(HBM, HBM),
        scratch=[state, held, held, pltpu.SemaphoreType.DMA((2 * heads,))],
    )
    return normed, grad_q, grad_k, grad_v


def solution(mesh):
    placed = (P("ctx", "tp"), P("ctx", "tp"), P("ctx", "tp"), P("tp"), P("ctx", "tp"))
    return jax.shard_map(
        on_device,
        mesh=mesh,
        in_specs=placed,
        out_specs=(P("ctx", "tp"), P("ctx", "tp"), P("ctx", "tp"), P("ctx", "tp")),
        check_vma=False,
    )
```

profile of v0, /device:TPU:0, one launch (start us, length us, event | category | flops | bytes accessed | tf_op | source)
XLA Modules:
  0.0 40.4 jit_solution(17269217088235544088)
XLA Ops:
  0.6 1.2 %shard_map.84 = (bf16[256,256]{1,0:T(8,128)(2,1)S(1)}, bf16[256,256]{1,0:T(8,128)(2,1)S(1)}, f32[64,128]{1,0:T(8,128)S(1)}, f32[64,128]{1,0:T(8,128)S(1)}, f32[6...) custom-call(bf16[256,256]{1,0:T(8,128)(2,1)} %k_hbm.1, ...), custom_call_target="tpu_custom_call" | custom-call | flops 10000000 | bytes 262144 | tf_op jit(solution)/shard_map/pallas_call | solution.py:35
  1.8 3.5 %collective-permute-start = (f32[64,128]{1,0:T(8,128)S(1)}, f32[64,128]{1,0:T(8,128)S(1)}, u32[]{:S(2)}, u32[]{:S(2)}) collective-permute-start(f32[64,128]{1,0:T(8,128)S(1)} %get-tuple-element.59), channel_id=1, source_target_pairs={{0,13},{1,12},{2,15},{3,14},{4,9},{5,8},{6,11},{7,10},{8,5},{9,4},... | collective-permute-start | bytes 98312 | tf_op jit(solution)/shard_map/ppermute | solution.py:251
  5.3 0.7 %collective-permute-start.1 = (f32[64,128]{1,0:T(8,128)S(1)}, f32[64,128]{1,0:T(8,128)S(1)}, u32[]{:S(2)}, u32[]{:S(2)}) collective-permute-start(f32[64,128]{1,0:T(8,128)S(1)} %get-tuple-element.60), channel_id=1, source_target_pairs={{0,9},{1,8},{2,11},{3,10},{4,13},{5,12},{6,15},{7,14},{8,1},{9,0},... | collective-permute-start | bytes 98312 | tf_op jit(solution)/shard_map/ppermute | solution.py:251
  6.2 0.5 %collective-permute-start.8 = (f32[64,128]{1,0:T(8,128)S(1)}, f32[64,128]{1,0:T(8,128)S(1)}, u32[]{:S(2)}, u32[]{:S(2)}) collective-permute-start(f32[64,128]{1,0:T(8,128)S(1)} %get-tuple-element.67), channel_id=1, source_target_pairs={{0,1},{1,0},{2,3},{3,2},{4,5},{5,4},{6,7},{7,6},{8,9},{9,8},{10,11... | collective-permute-start | bytes 98312 | tf_op jit(solution)/shard_map/ppermute | solution.py:251
  7.1 0.5 %collective-permute-start.9 = (f32[64,128]{1,0:T(8,128)S(1)}, f32[64,128]{1,0:T(8,128)S(1)}, u32[]{:S(2)}, u32[]{:S(2)}) collective-permute-start(f32[64,128]{1,0:T(8,128)S(1)} %get-tuple-element.69), channel_id=1, source_target_pairs={{0,1},{1,0},{2,3},{3,2},{4,5},{5,4},{6,7},{7,6},{8,9},{9,8},{10,11... | collective-permute-start | bytes 98312 | tf_op jit(solution)/shard_map/ppermute | solution.py:251
  7.6 1.1 %collective-permute-done.1.refs_1_ = f32[64,128]{1,0:T(8,128)S(1)} collective-permute-done((f32[64,128]{1,0:T(8,128)S(1)}, f32[64,128]{1,0:T(8,128)S(1)}, u32[]{:S(2)}, u32[]{:S(2)}) %collective-permute-start.1) | collective-permute-done | bytes 32800 | tf_op jit(solution)/shard_map/ppermute | solution.py:251
  8.6 1.0 %collective-permute-done.2.refs_2_ = f32[64,128]{1,0:T(8,128)S(1)} collective-permute-done((f32[64,128]{1,0:T(8,128)S(1)}, f32[64,128]{1,0:T(8,128)S(1)}, u32[]{:S(2)}, u32[]{:S(2)}) %collective-permute-start.2) | collective-permute-done | bytes 32800 | tf_op jit(solution)/shard_map/ppermute | solution.py:251
  9.9 1.9 %collective-permute-start.4 = (f32[64,128]{1,0:T(8,128)S(1)}, f32[64,128]{1,0:T(8,128)S(1)}, u32[]{:S(2)}, u32[]{:S(2)}) collective-permute-start(f32[64,128]{1,0:T(8,128)S(1)} %get-tuple-element.63), channel_id=1, source_target_pairs={{0,13},{1,4},{2,15},{3,6},{4,9},{5,0},{6,11},{7,2},{8,5},{9,12},{1... | collective-permute-start | bytes 98312 | tf_op jit(solution)/shard_map/ppermute | solution.py:251
  11.8 0.9 %collective-permute-start.5 = (f32[64,128]{1,0:T(8,128)S(1)}, f32[64,128]{1,0:T(8,128)S(1)}, u32[]{:S(2)}, u32[]{:S(2)}) collective-permute-start(f32[64,128]{1,0:T(8,128)S(1)} %get-tuple-element.64), channel_id=1, source_target_pairs={{0,9},{1,12},{2,11},{3,14},{4,13},{5,8},{6,15},{7,10},{8,1},{9,4},... | collective-permute-start | bytes 98312 | tf_op jit(solution)/shard_map/ppermute | solution.py:251
  12.7 0.7 %collective-permute-start.6 = (f32[64,128]{1,0:T(8,128)S(1)}, f32[64,128]{1,0:T(8,128)S(1)}, u32[]{:S(2)}, u32[]{:S(2)}) collective-permute-start(f32[64,128]{1,0:T(8,128)S(1)} %get-tuple-element.65), channel_id=1, source_target_pairs={{0,5},{1,8},{2,7},{3,10},{4,1},{5,12},{6,3},{7,14},{8,13},{9,0},{1... | collective-permute-start | bytes 98312 | tf_op jit(solution)/shard_map/ppermute | solution.py:251
  13.5 1.1 %collective-permute-done.10.refs_4_ = f32[64,128]{1,0:T(8,128)S(1)} collective-permute-done((f32[64,128]{1,0:T(8,128)S(1)}, f32[64,128]{1,0:T(8,128)S(1)}, u32[]{:S(2)}, u32[]{:S(2)}) %collective-permute-start.10) | collective-permute-done | bytes 32800 | tf_op jit(solution)/shard_map/ppermute | solution.py:283
  15.1 1.0 %collective-permute-done.5.refs_1_ = f32[64,128]{1,0:T(8,128)S(1)} collective-permute-done((f32[64,128]{1,0:T(8,128)S(1)}, f32[64,128]{1,0:T(8,128)S(1)}, u32[]{:S(2)}, u32[]{:S(2)}) %collective-permute-start.5) | collective-permute-done | bytes 32800 | tf_op jit(solution)/shard_map/ppermute | solution.py:251
  16.1 0.5 %collective-permute-start.14 = (f32[64,128]{1,0:T(8,128)S(1)}, f32[64,128]{1,0:T(8,128)S(1)}, u32[]{:S(2)}, u32[]{:S(2)}) collective-permute-start(f32[64,128]{1,0:T(8,128)S(1)} %get-tuple-element.75), channel_id=1, source_target_pairs={{0,1},{1,0},{2,3},{3,2},{4,5},{5,4},{6,7},{7,6},{8,9},{9,8},{10,11... | collective-permute-start | bytes 98312 | tf_op jit(solution)/shard_map/ppermute | solution.py:251
  16.6 1.5 %shard_map.85 = (bf16[2,256,256]{2,1,0:T(8,128)(2,1)S(1)}, f32[256,256]{1,0:T(8,128)S(1)}, bf16[256,256]{1,0:T(8,128)(2,1)S(1)}, bf16[256,256]{1,0:T(8,128)(2,1)...) custom-call(bf16[256,256]{1,0:T(8,128)(2,1)S(1)} %get-tuple-element.54.k, bf16[256,256]{1,0:T(8,128)(2,1)S(1)} %get-tuple-element.55.v, ...), custom_call_target="tpu_custom_call" | custom-call | flops 67108864 | bytes 525312 | tf_op jit(solution)/shard_map/pallas_call | solution.py:35
  18.5 1.6 %collective-permute-start.17 = (f32[2,256]{1,0:T(2,128)S(1)}, f32[2,256]{1,0:T(2,128)S(1)}, u32[]{:S(2)}, u32[]{:S(2)}) collective-permute-start(f32[2,256]{1,0:T(2,128)S(1)} %get-tuple-element.78.refs_0_), channel_id=1, source_target_pairs={{0,2},{1,3},{2,0},{3,1},{4,6},{5,7},{6,4},{7,5},{8,10},{9,11},{10,... | collective-permute-start | bytes 6152 | tf_op jit(solution)/shard_map/ppermute | solution.py:303
  20.1 0.6 %collective-permute-start.15 = (f32[2,256]{1,0:T(2,128)S(1)}, f32[2,256]{1,0:T(2,128)S(1)}, u32[]{:S(2)}, u32[]{:S(2)}) collective-permute-start(f32[2,256]{1,0:T(2,128)S(1)} %get-tuple-element.78.refs_0_), channel_id=1, source_target_pairs={{0,1},{1,0},{2,3},{3,2},{4,5},{5,4},{6,7},{7,6},{8,9},{9,8},{10,11... | collective-permute-start | bytes 6152 | tf_op jit(solution)/shard_map/ppermute | solution.py:303
  20.7 1.4 %collective-permute-done.17.refs_3_ = f32[2,256]{1,0:T(2,128)S(1)} collective-permute-done((f32[2,256]{1,0:T(2,128)S(1)}, f32[2,256]{1,0:T(2,128)S(1)}, u32[]{:S(2)}, u32[]{:S(2)}) %collective-permute-start.17) | collective-permute-done | bytes 2080 | tf_op jit(solution)/shard_map/ppermute | solution.py:303
  22.1 0.9 %collective-permute-done.16.refs_2_ = f32[2,256]{1,0:T(2,128)S(1)} collective-permute-done((f32[2,256]{1,0:T(2,128)S(1)}, f32[2,256]{1,0:T(2,128)S(1)}, u32[]{:S(2)}, u32[]{:S(2)}) %collective-permute-start.16) | collective-permute-done | bytes 2080 | tf_op jit(solution)/shard_map/ppermute | solution.py:303
  23.4 1.0 %collective-permute-start.18 = (f32[64,128]{1,0:T(8,128)S(1)}, f32[64,128]{1,0:T(8,128)S(1)}, u32[]{:S(2)}, u32[]{:S(2)}) collective-permute-start(f32[64,128]{1,0:T(8,128)S(1)} %get-tuple-element.88), channel_id=1, source_target_pairs={{0,13},{1,12},{2,15},{3,14},{4,9},{5,8},{6,11},{7,10},{8,5},{9,4},... | collective-permute-start | bytes 98312 | tf_op jit(solution)/shard_map/ppermute | solution.py:251
  24.4 1.1 %collective-permute-start.19 = (f32[64,128]{1,0:T(8,128)S(1)}, f32[64,128]{1,0:T(8,128)S(1)}, u32[]{:S(2)}, u32[]{:S(2)}) collective-permute-start(f32[64,128]{1,0:T(8,128)S(1)} %get-tuple-element.89), channel_id=1, source_target_pairs={{0,9},{1,8},{2,11},{3,10},{4,13},{5,12},{6,15},{7,14},{8,1},{9,0},... | collective-permute-start | bytes 98312 | tf_op jit(solution)/shard_map/ppermute | solution.py:251
  25.5 0.5 %collective-permute-start.20 = (f32[64,128]{1,0:T(8,128)S(1)}, f32[64,128]{1,0:T(8,128)S(1)}, u32[]{:S(2)}, u32[]{:S(2)}) collective-permute-start(f32[64,128]{1,0:T(8,128)S(1)} %get-tuple-element.90), channel_id=1, source_target_pairs={{0,5},{1,4},{2,7},{3,6},{4,1},{5,0},{6,3},{7,2},{8,13},{9,12},{10,... | collective-permute-start | bytes 98312 | tf_op jit(solution)/shard_map/ppermute | solution.py:251
  26.0 0.8 %collective-permute-start.21 = (f32[64,128]{1,0:T(8,128)S(1)}, f32[64,128]{1,0:T(8,128)S(1)}, u32[]{:S(2)}, u32[]{:S(2)}) collective-permute-start(f32[64,128]{1,0:T(8,128)S(1)} %get-tuple-element.91), channel_id=1, source_target_pairs={{0,1},{1,0},{2,3},{3,2},{4,5},{5,4},{6,7},{7,6},{8,9},{9,8},{10,11... | collective-permute-start | bytes 98312 | tf_op jit(solution)/shard_map/ppermute | solution.py:251
  26.8 1.2 %collective-permute-done.18.refs_0_ = f32[64,128]{1,0:T(8,128)S(1)} collective-permute-done((f32[64,128]{1,0:T(8,128)S(1)}, f32[64,128]{1,0:T(8,128)S(1)}, u32[]{:S(2)}, u32[]{:S(2)}) %collective-permute-start.18) | collective-permute-done | bytes 32800 | tf_op jit(solution)/shard_map/ppermute | solution.py:251
  28.0 1.2 %collective-permute-done.20.refs_2_ = f32[64,128]{1,0:T(8,128)S(1)} collective-permute-done((f32[64,128]{1,0:T(8,128)S(1)}, f32[64,128]{1,0:T(8,128)S(1)}, u32[]{:S(2)}, u32[]{:S(2)}) %collective-permute-start.20) | collective-permute-done | bytes 32800 | tf_op jit(solution)/shard_map/ppermute | solution.py:251
  29.2 2.8 %collective-permute-start.22 = (f32[64,128]{1,0:T(8,128)S(1)}, f32[64,128]{1,0:T(8,128)S(1)}, u32[]{:S(2)}, u32[]{:S(2)}) collective-permute-start(f32[64,128]{1,0:T(8,128)S(1)} %get-tuple-element.93), channel_id=1, source_target_pairs={{0,16},{4,20},{8,24},{12,28},{16,0},{20,4},{24,8},{28,12},{1,17},{... | collective-permute-start | bytes 98312 | tf_op jit(solution)/shard_map/ppermute | solution.py:283
  31.9 0.5 %collective-permute-start.28 = (f32[64,128]{1,0:T(8,128)S(1)}, f32[64,128]{1,0:T(8,128)S(1)}, u32[]{:S(2)}, u32[]{:S(2)}) collective-permute-start(f32[64,128]{1,0:T(8,128)S(1)} %get-tuple-element.99), channel_id=1, source_target_pairs={{0,1},{1,0},{2,3},{3,2},{4,5},{5,4},{6,7},{7,6},{8,9},{9,8},{10,11... | collective-permute-start | bytes 98312 | tf_op jit(solution)/shard_map/ppermute | solution.py:251
  32.5 0.5 %collective-permute-start.30 = (f32[64,128]{1,0:T(8,128)S(1)}, f32[64,128]{1,0:T(8,128)S(1)}, u32[]{:S(2)}, u32[]{:S(2)}) collective-permute-start(f32[64,128]{1,0:T(8,128)S(1)} %get-tuple-element.101), channel_id=1, source_target_pairs={{0,1},{1,0},{2,3},{3,2},{4,5},{5,4},{6,7},{7,6},{8,9},{9,8},{10,11... | collective-permute-start | bytes 98312 | tf_op jit(solution)/shard_map/ppermute | solution.py:251
  33.0 1.2 %collective-permute-done.22.over = f32[64,128]{1,0:T(8,128)S(1)} collective-permute-done((f32[64,128]{1,0:T(8,128)S(1)}, f32[64,128]{1,0:T(8,128)S(1)}, u32[]{:S(2)}, u32[]{:S(2)}) %collective-permute-start.22) | collective-permute-done | bytes 32800 | tf_op jit(solution)/shard_map/ppermute | solution.py:283
  34.3 1.8 %collective-permute-start.24 = (f32[64,128]{1,0:T(8,128)S(1)}, f32[64,128]{1,0:T(8,128)S(1)}, u32[]{:S(2)}, u32[]{:S(2)}) collective-permute-start(f32[64,128]{1,0:T(8,128)S(1)} %get-tuple-element.95), channel_id=1, source_target_pairs={{0,9},{1,12},{2,11},{3,14},{4,13},{5,8},{6,15},{7,10},{8,1},{9,4},... | collective-permute-start | bytes 98312 | tf_op jit(solution)/shard_map/ppermute | solution.py:251
  36.1 1.5 %collective-permute-start.25 = (f32[64,128]{1,0:T(8,128)S(1)}, f32[64,128]{1,0:T(8,128)S(1)}, u32[]{:S(2)}, u32[]{:S(2)}) collective-permute-start(f32[64,128]{1,0:T(8,128)S(1)} %get-tuple-element.96), channel_id=1, source_target_pairs={{0,5},{1,8},{2,7},{3,10},{4,1},{5,12},{6,3},{7,14},{8,13},{9,0},{1... | collective-permute-start | bytes 98312 | tf_op jit(solution)/shard_map/ppermute | solution.py:251
  37.6 1.4 %shard_map.90 = (bf16[256,256]{1,0:T(8,128)(2,1)}, bf16[256,256]{1,0:T(8,128)(2,1)}, f32[256,256]{1,0:T(8,128)S(1)}, f32[256,256]{1,0:T(8,128)S(1)}) custom-call(bf16[256,256]{1,0:T(8,128)(2,1)S(1)} %get-tuple-element.79.ga, bf16[256,256]{1,0:T(8,128)(2,1)S(1)} %get-tuple-element.56.q, bf16[256,256]{1,0:T(8,128)(2,1)S(1)} %get-tuple-element.54.k, ...), custom_call_target="tpu_custom_call" | custom-call | flops 150994944 | bytes 1311744 | tf_op jit(solution)/shard_map/pallas_call | solution.py:35
  39.5 0.9 %shard_map.93 = (bf16[256,256]{1,0:T(8,128)(2,1)}, bf16[256,256]{1,0:T(8,128)(2,1)}) custom-call(bf16[256,256]{1,0:T(8,128)(2,1)S(1)} %get-tuple-element.54.k, bf16[256,256]{1,0:T(8,128)(2,1)S(1)} %get-tuple-element.55.v, f32[256,256]{1,0:T(8,128)S(1)} %get-tuple-element.86.gk_part, f32[256,256]{1,0:T(8,128)S(1)} %get-tuple-element.87.gv_part, ...), custom_call_target="tpu_custom_call" | custom-call | flops 10000000 | bytes 1048576 | tf_op jit(solution)/shard_map/pallas_call | solution.py:35
  (40 shorter events, 2.8 us)
Async XLA Ops:
  1.8 5.2 %collective-permute-start = (f32[64,128]{1,0:T(8,128)S(1)}, f32[64,128]{1,0:T(8,128)S(1)}, u32[]{:S(2)}, u32[]{:S(2)}) collective-permute-start(f32[64,128]{1,0:T(8,128)S(1)} %get-tuple-element.59), channel_id=1, source_target_pairs={{0,13},{1,12},{2,15},{3,14},{4,9},{5,8},{6,11},{7,10},{8,5},{9,4},... | collective-permute-start | bytes 98312 | tf_op jit(solution)/shard_map/ppermute | solution.py:251
  5.3 3.3 %collective-permute-start.1 = (f32[64,128]{1,0:T(8,128)S(1)}, f32[64,128]{1,0:T(8,128)S(1)}, u32[]{:S(2)}, u32[]{:S(2)}) collective-permute-start(f32[64,128]{1,0:T(8,128)S(1)} %get-tuple-element.60), channel_id=1, source_target_pairs={{0,9},{1,8},{2,11},{3,10},{4,13},{5,12},{6,15},{7,14},{8,1},{9,0},... | collective-permute-start | bytes 98312 | tf_op jit(solution)/shard_map/ppermute | solution.py:251
  6.0 3.6 %collective-permute-start.2 = (f32[64,128]{1,0:T(8,128)S(1)}, f32[64,128]{1,0:T(8,128)S(1)}, u32[]{:S(2)}, u32[]{:S(2)}) collective-permute-start(f32[64,128]{1,0:T(8,128)S(1)} %get-tuple-element.61), channel_id=1, source_target_pairs={{0,5},{1,4},{2,7},{3,6},{4,1},{5,0},{6,3},{7,2},{8,13},{9,12},{10,... | collective-permute-start | bytes 98312 | tf_op jit(solution)/shard_map/ppermute | solution.py:251
  6.2 3.4 %collective-permute-start.3 = (f32[64,128]{1,0:T(8,128)S(1)}, f32[64,128]{1,0:T(8,128)S(1)}, u32[]{:S(2)}, u32[]{:S(2)}) collective-permute-start(f32[64,128]{1,0:T(8,128)S(1)} %get-tuple-element.62), channel_id=1, source_target_pairs={{0,1},{1,0},{2,3},{3,2},{4,5},{5,4},{6,7},{7,6},{8,9},{9,8},{10,11... | collective-permute-start | bytes 98312 | tf_op jit(solution)/shard_map/ppermute | solution.py:251
  6.2 6.5 %collective-permute-start.8 = (f32[64,128]{1,0:T(8,128)S(1)}, f32[64,128]{1,0:T(8,128)S(1)}, u32[]{:S(2)}, u32[]{:S(2)}) collective-permute-start(f32[64,128]{1,0:T(8,128)S(1)} %get-tuple-element.67), channel_id=1, source_target_pairs={{0,1},{1,0},{2,3},{3,2},{4,5},{5,4},{6,7},{7,6},{8,9},{9,8},{10,11... | collective-permute-start | bytes 98312 | tf_op jit(solution)/shard_map/ppermute | solution.py:251
  7.1 6.4 %collective-permute-start.9 = (f32[64,128]{1,0:T(8,128)S(1)}, f32[64,128]{1,0:T(8,128)S(1)}, u32[]{:S(2)}, u32[]{:S(2)}) collective-permute-start(f32[64,128]{1,0:T(8,128)S(1)} %get-tuple-element.69), channel_id=1, source_target_pairs={{0,1},{1,0},{2,3},{3,2},{4,5},{5,4},{6,7},{7,6},{8,9},{9,8},{10,11... | collective-permute-start | bytes 98312 | tf_op jit(solution)/shard_map/ppermute | solution.py:251
  9.6 4.9 %collective-permute-start.10 = (f32[64,128]{1,0:T(8,128)S(1)}, f32[64,128]{1,0:T(8,128)S(1)}, u32[]{:S(2)}, u32[]{:S(2)}) collective-permute-start(f32[64,128]{1,0:T(8,128)S(1)} %get-tuple-element.71), channel_id=1, source_target_pairs={{0,16},{4,20},{8,24},{12,28},{16,0},{20,4},{24,8},{28,12},{1,17},{... | collective-permute-start | bytes 98312 | tf_op jit(solution)/shard_map/ppermute | solution.py:283
  9.9 4.7 %collective-permute-start.4 = (f32[64,128]{1,0:T(8,128)S(1)}, f32[64,128]{1,0:T(8,128)S(1)}, u32[]{:S(2)}, u32[]{:S(2)}) collective-permute-start(f32[64,128]{1,0:T(8,128)S(1)} %get-tuple-element.63), channel_id=1, source_target_pairs={{0,13},{1,4},{2,15},{3,6},{4,9},{5,0},{6,11},{7,2},{8,5},{9,12},{1... | collective-permute-start | bytes 98312 | tf_op jit(solution)/shard_map/ppermute | solution.py:251
  11.8 4.3 %collective-permute-start.5 = (f32[64,128]{1,0:T(8,128)S(1)}, f32[64,128]{1,0:T(8,128)S(1)}, u32[]{:S(2)}, u32[]{:S(2)}) collective-permute-start(f32[64,128]{1,0:T(8,128)S(1)} %get-tuple-element.64), channel_id=1, source_target_pairs={{0,9},{1,12},{2,11},{3,14},{4,13},{5,8},{6,15},{7,10},{8,1},{9,4},... | collective-permute-start | bytes 98312 | tf_op jit(solution)/shard_map/ppermute | solution.py:251
  12.7 3.4 %collective-permute-start.6 = (f32[64,128]{1,0:T(8,128)S(1)}, f32[64,128]{1,0:T(8,128)S(1)}, u32[]{:S(2)}, u32[]{:S(2)}) collective-permute-start(f32[64,128]{1,0:T(8,128)S(1)} %get-tuple-element.65), channel_id=1, source_target_pairs={{0,5},{1,8},{2,7},{3,10},{4,1},{5,12},{6,3},{7,14},{8,13},{9,0},{1... | collective-permute-start | bytes 98312 | tf_op jit(solution)/shard_map/ppermute | solution.py:251
  13.5 4.6 %collective-permute-start.7 = (f32[64,128]{1,0:T(8,128)S(1)}, f32[64,128]{1,0:T(8,128)S(1)}, u32[]{:S(2)}, u32[]{:S(2)}) collective-permute-start(f32[64,128]{1,0:T(8,128)S(1)} %get-tuple-element.66), channel_id=1, source_target_pairs={{0,1},{1,0},{2,3},{3,2},{4,5},{5,4},{6,7},{7,6},{8,9},{9,8},{10,11... | collective-permute-start | bytes 98312 | tf_op jit(solution)/shard_map/ppermute | solution.py:251
  14.6 3.5 %collective-permute-start.11 = (f32[64,128]{1,0:T(8,128)S(1)}, f32[64,128]{1,0:T(8,128)S(1)}, u32[]{:S(2)}, u32[]{:S(2)}) collective-permute-start(f32[64,128]{1,0:T(8,128)S(1)} %get-tuple-element.72), channel_id=1, source_target_pairs={{0,1},{1,0},{2,3},{3,2},{4,5},{5,4},{6,7},{7,6},{8,9},{9,8},{10,11... | collective-permute-start | bytes 98312 | tf_op jit(solution)/shard_map/ppermute | solution.py:251
  14.6 3.5 %collective-permute-start.12 = (f32[64,128]{1,0:T(8,128)S(1)}, f32[64,128]{1,0:T(8,128)S(1)}, u32[]{:S(2)}, u32[]{:S(2)}) collective-permute-start(f32[64,128]{1,0:T(8,128)S(1)} %get-tuple-element.73), channel_id=1, source_target_pairs={{0,1},{1,0},{2,3},{3,2},{4,5},{5,4},{6,7},{7,6},{8,9},{9,8},{10,11... | collective-permute-start | bytes 98312 | tf_op jit(solution)/shard_map/ppermute | solution.py:251
  16.1 2.0 %collective-permute-start.13 = (f32[64,128]{1,0:T(8,128)S(1)}, f32[64,128]{1,0:T(8,128)S(1)}, u32[]{:S(2)}, u32[]{:S(2)}) collective-permute-start(f32[64,128]{1,0:T(8,128)S(1)} %get-tuple-element.74), channel_id=1, source_target_pairs={{0,1},{1,0},{2,3},{3,2},{4,5},{5,4},{6,7},{7,6},{8,9},{9,8},{10,11... | collective-permute-start | bytes 98312 | tf_op jit(solution)/shard_map/ppermute | solution.py:251
  16.1 2.0 %collective-permute-start.14 = (f32[64,128]{1,0:T(8,128)S(1)}, f32[64,128]{1,0:T(8,128)S(1)}, u32[]{:S(2)}, u32[]{:S(2)}) collective-permute-start(f32[64,128]{1,0:T(8,128)S(1)} %get-tuple-element.75), channel_id=1, source_target_pairs={{0,1},{1,0},{2,3},{3,2},{4,5},{5,4},{6,7},{7,6},{8,9},{9,8},{10,11... | collective-permute-start | bytes 98312 | tf_op jit(solution)/shard_map/ppermute | solution.py:251
  18.5 3.6 %collective-permute-start.17 = (f32[2,256]{1,0:T(2,128)S(1)}, f32[2,256]{1,0:T(2,128)S(1)}, u32[]{:S(2)}, u32[]{:S(2)}) collective-permute-start(f32[2,256]{1,0:T(2,128)S(1)} %get-tuple-element.78.refs_0_), channel_id=1, source_target_pairs={{0,2},{1,3},{2,0},{3,1},{4,6},{5,7},{6,4},{7,5},{8,10},{9,11},{10,... | collective-permute-start | bytes 6152 | tf_op jit(solution)/shard_map/ppermute | solution.py:303
  20.1 3.0 %collective-permute-start.16 = (f32[2,256]{1,0:T(2,128)S(1)}, f32[2,256]{1,0:T(2,128)S(1)}, u32[]{:S(2)}, u32[]{:S(2)}) collective-permute-start(f32[2,256]{1,0:T(2,128)S(1)} %get-tuple-element.78.refs_0_), channel_id=1, source_target_pairs={{0,3},{1,2},{2,1},{3,0},{4,7},{5,6},{6,5},{7,4},{8,11},{9,10},{10,... | collective-permute-start | bytes 6152 | tf_op jit(solution)/shard_map/ppermute | solution.py:303
  20.1 3.0 %collective-permute-start.15 = (f32[2,256]{1,0:T(2,128)S(1)}, f32[2,256]{1,0:T(2,128)S(1)}, u32[]{:S(2)}, u32[]{:S(2)}) collective-permute-start(f32[2,256]{1,0:T(2,128)S(1)} %get-tuple-element.78.refs_0_), channel_id=1, source_target_pairs={{0,1},{1,0},{2,3},{3,2},{4,5},{5,4},{6,7},{7,6},{8,9},{9,8},{10,11... | collective-permute-start | bytes 6152 | tf_op jit(solution)/shard_map/ppermute | solution.py:303
  23.4 4.6 %collective-permute-start.18 = (f32[64,128]{1,0:T(8,128)S(1)}, f32[64,128]{1,0:T(8,128)S(1)}, u32[]{:S(2)}, u32[]{:S(2)}) collective-permute-start(f32[64,128]{1,0:T(8,128)S(1)} %get-tuple-element.88), channel_id=1, source_target_pairs={{0,13},{1,12},{2,15},{3,14},{4,9},{5,8},{6,11},{7,10},{8,5},{9,4},... | collective-permute-start | bytes 98312 | tf_op jit(solution)/shard_map/ppermute | solution.py:251
  24.4 3.6 %collective-permute-start.19 = (f32[64,128]{1,0:T(8,128)S(1)}, f32[64,128]{1,0:T(8,128)S(1)}, u32[]{:S(2)}, u32[]{:S(2)}) collective-permute-start(f32[64,128]{1,0:T(8,128)S(1)} %get-tuple-element.89), channel_id=1, source_target_pairs={{0,9},{1,8},{2,11},{3,10},{4,13},{5,12},{6,15},{7,14},{8,1},{9,0},... | collective-permute-start | bytes 98312 | tf_op jit(solution)/shard_map/ppermute | solution.py:251
  25.5 3.7 %collective-permute-start.20 = (f32[64,128]{1,0:T(8,128)S(1)}, f32[64,128]{1,0:T(8,128)S(1)}, u32[]{:S(2)}, u32[]{:S(2)}) collective-permute-start(f32[64,128]{1,0:T(8,128)S(1)} %get-tuple-element.90), channel_id=1, source_target_pairs={{0,5},{1,4},{2,7},{3,6},{4,1},{5,0},{6,3},{7,2},{8,13},{9,12},{10,... | collective-permute-start | bytes 98312 | tf_op jit(solution)/shard_map/ppermute | solution.py:251
  26.0 3.1 %collective-permute-start.21 = (f32[64,128]{1,0:T(8,128)S(1)}, f32[64,128]{1,0:T(8,128)S(1)}, u32[]{:S(2)}, u32[]{:S(2)}) collective-permute-start(f32[64,128]{1,0:T(8,128)S(1)} %get-tuple-element.91), channel_id=1, source_target_pairs={{0,1},{1,0},{2,3},{3,2},{4,5},{5,4},{6,7},{7,6},{8,9},{9,8},{10,11... | collective-permute-start | bytes 98312 | tf_op jit(solution)/shard_map/ppermute | solution.py:251
  29.2 5.0 %collective-permute-start.22 = (f32[64,128]{1,0:T(8,128)S(1)}, f32[64,128]{1,0:T(8,128)S(1)}, u32[]{:S(2)}, u32[]{:S(2)}) collective-permute-start(f32[64,128]{1,0:T(8,128)S(1)} %get-tuple-element.93), channel_id=1, source_target_pairs={{0,16},{4,20},{8,24},{12,28},{16,0},{20,4},{24,8},{28,12},{1,17},{... | collective-permute-start | bytes 98312 | tf_op jit(solution)/shard_map/ppermute | solution.py:283
  31.9 2.4 %collective-permute-start.27 = (f32[64,128]{1,0:T(8,128)S(1)}, f32[64,128]{1,0:T(8,128)S(1)}, u32[]{:S(2)}, u32[]{:S(2)}) collective-permute-start(f32[64,128]{1,0:T(8,128)S(1)} %get-tuple-element.98), channel_id=1, source_target_pairs={{0,1},{1,0},{2,3},{3,2},{4,5},{5,4},{6,7},{7,6},{8,9},{9,8},{10,11... | collective-permute-start | bytes 98312 | tf_op jit(solution)/shard_map/ppermute | solution.py:251
  31.9 4.2 %collective-permute-start.28 = (f32[64,128]{1,0:T(8,128)S(1)}, f32[64,128]{1,0:T(8,128)S(1)}, u32[]{:S(2)}, u32[]{:S(2)}) collective-permute-start(f32[64,128]{1,0:T(8,128)S(1)} %get-tuple-element.99), channel_id=1, source_target_pairs={{0,1},{1,0},{2,3},{3,2},{4,5},{5,4},{6,7},{7,6},{8,9},{9,8},{10,11... | collective-permute-start | bytes 98312 | tf_op jit(solution)/shard_map/ppermute | solution.py:251
  32.4 5.2 %collective-permute-start.29 = (f32[64,128]{1,0:T(8,128)S(1)}, f32[64,128]{1,0:T(8,128)S(1)}, u32[]{:S(2)}, u32[]{:S(2)}) collective-permute-start(f32[64,128]{1,0:T(8,128)S(1)} %get-tuple-element.100), channel_id=1, source_target_pairs={{0,1},{1,0},{2,3},{3,2},{4,5},{5,4},{6,7},{7,6},{8,9},{9,8},{10,11... | collective-permute-start | bytes 98312 | tf_op jit(solution)/shard_map/ppermute | solution.py:251
  32.5 6.5 %collective-permute-start.30 = (f32[64,128]{1,0:T(8,128)S(1)}, f32[64,128]{1,0:T(8,128)S(1)}, u32[]{:S(2)}, u32[]{:S(2)}) collective-permute-start(f32[64,128]{1,0:T(8,128)S(1)} %get-tuple-element.101), channel_id=1, source_target_pairs={{0,1},{1,0},{2,3},{3,2},{4,5},{5,4},{6,7},{7,6},{8,9},{9,8},{10,11... | collective-permute-start | bytes 98312 | tf_op jit(solution)/shard_map/ppermute | solution.py:251
  34.2 4.8 %collective-permute-start.23 = (f32[64,128]{1,0:T(8,128)S(1)}, f32[64,128]{1,0:T(8,128)S(1)}, u32[]{:S(2)}, u32[]{:S(2)}) collective-permute-start(f32[64,128]{1,0:T(8,128)S(1)} %get-tuple-element.94), channel_id=1, source_target_pairs={{0,13},{1,4},{2,15},{3,6},{4,9},{5,0},{6,11},{7,2},{8,5},{9,12},{1... | collective-permute-start | bytes 98312 | tf_op jit(solution)/shard_map/ppermute | solution.py:251
  34.3 4.7 %collective-permute-start.24 = (f32[64,128]{1,0:T(8,128)S(1)}, f32[64,128]{1,0:T(8,128)S(1)}, u32[]{:S(2)}, u32[]{:S(2)}) collective-permute-start(f32[64,128]{1,0:T(8,128)S(1)} %get-tuple-element.95), channel_id=1, source_target_pairs={{0,9},{1,12},{2,11},{3,14},{4,13},{5,8},{6,15},{7,10},{8,1},{9,4},... | collective-permute-start | bytes 98312 | tf_op jit(solution)/shard_map/ppermute | solution.py:251
  36.1 3.4 %collective-permute-start.25 = (f32[64,128]{1,0:T(8,128)S(1)}, f32[64,128]{1,0:T(8,128)S(1)}, u32[]{:S(2)}, u32[]{:S(2)}) collective-permute-start(f32[64,128]{1,0:T(8,128)S(1)} %get-tuple-element.96), channel_id=1, source_target_pairs={{0,5},{1,8},{2,7},{3,10},{4,1},{5,12},{6,3},{7,14},{8,13},{9,0},{1... | collective-permute-start | bytes 98312 | tf_op jit(solution)/shard_map/ppermute | solution.py:251
  37.6 1.9 %collective-permute-start.26 = (f32[64,128]{1,0:T(8,128)S(1)}, f32[64,128]{1,0:T(8,128)S(1)}, u32[]{:S(2)}, u32[]{:S(2)}) collective-permute-start(f32[64,128]{1,0:T(8,128)S(1)} %get-tuple-element.97), channel_id=1, source_target_pairs={{0,1},{1,0},{2,3},{3,2},{4,5},{5,4},{6,7},{7,6},{8,9},{9,8},{10,11... | collective-permute-start | bytes 98312 | tf_op jit(solution)/shard_map/ppermute | solution.py:251
where the time goes:
time: 40.6 us; the launch traced here: 40.4 us
  starting transfers between devices  23 us (57%)
  waiting for transfers between devices  10.9 us (27%)
  Pallas kernels  5.79 us (14%)
  between operations  0.76 us (2%)
    ppermute x26, starting transfers between devices, exchange(): return lax.ppermute(piece, ('ctx', 'tp'), pairs)  17.8 us
    ppermute x26, waiting for transfers between devices, exchange(): return lax.ppermute(piece, ('ctx', 'tp'), pairs)  6.17 us
    pallas_call x10, Pallas kernels, call(): pl.pallas_call(body, out_shape=outs, in_specs=ins or [VMEM] * len(args),...  5.79 us
    ppermute x2, starting transfers between devices, carried_in(): over = lax.ppermute(total, 'ctx', [(j, j ^ group) for j in both])  3.03 us
    ppermute x3, waiting for transfers between devices, from_all(): lax.ppermute(part, axis, [(i, i ^ step if even else (i + step) % count) f...  2.39 us
    ppermute x2, waiting for transfers between devices, carried_in(): over = lax.ppermute(total, 'ctx', [(j, j ^ group) for j in both])  2.29 us
    ppermute x3, starting transfers between devices, from_all(): lax.ppermute(part, axis, [(i, i ^ step if even else (i + step) % count) f...  2.2 us
  transfers between devices with their start and end apart: 31, of which 11 were waited for; matrix products, arithmetic and copies ran while one was open for 0% of the time, Pallas kernels for 7%

commit v1 on v0

--- a/solution.py
+++ b/solution.py
@@ -62,7 +62,7 @@
     return (
         (3, 2, 1, 0),
         (3, 2, 1, 0),
-        (3 - 2 * odd, 2 + odd, 1 + odd, 0),
+        (3 - odd, 1 + 2 * odd, 2 - odd, 0),
     )[order][i]
 
 

time: 40.6 us -> 40.7 us (level)
    ppermute x2, waiting for transfers between devices: 2.29 us -> 1.68 us  [carried_in(): over = lax.ppermute(total, 'ctx', [(j, j ^ group) for j in both])]
  transfers between devices with their start and end apart: 31 -> 31, of which waited for: 11 -> 12; matrix products, arithmetic and copies ran while one was open for 0% -> 0% of each run, Pallas kernels for 7% -> 7%
where the time goes in v1:
time: 40.7 us; the launch traced here: 40.5 us
  starting transfers between devices  23.4 us (57%)
  waiting for transfers between devices  10.5 us (26%)
  Pallas kernels  5.79 us (14%)
  between operations  0.77 us (2%)
    ppermute x26, starting transfers between devices, exchange(): return lax.ppermute(piece, ('ctx', 'tp'), pairs)  17.7 us
    ppermute x26, waiting for transfers between devices, exchange(): return lax.ppermute(piece, ('ctx', 'tp'), pairs)  6.48 us
    pallas_call x10, Pallas kernels, call(): pl.pallas_call(body, out_shape=outs, in_specs=ins or [VMEM] * len(args),...  5.79 us
    ppermute x2, starting transfers between devices, carried_in(): over = lax.ppermute(total, 'ctx', [(j, j ^ group) for j in both])  3.44 us
    ppermute x3, waiting for transfers between devices, from_all(): lax.ppermute(part, axis, [(i, i ^ step if even else (i + step) % count) f...  2.39 us
    ppermute x3, starting transfers between devices, from_all(): lax.ppermute(part, axis, [(i, i ^ step if even else (i + step) % count) f...  2.2 us
    ppermute x2, waiting for transfers between devices, carried_in(): over = lax.ppermute(total, 'ctx', [(j, j ^ group) for j in both])  1.68 us
  transfers between devices with their start and end apart: 31, of which 12 were waited for; matrix products, arithmetic and copies ran while one was open for 0% of the time, Pallas kernels for 7%

profile of v1, /device:TPU:0, one launch (start us, length us, event | category | flops | bytes accessed | tf_op | source)
XLA Modules:
  0.0 40.5 jit_solution(17400321591023211462)
XLA Ops:
  0.6 1.2 %shard_map.84 = (bf16[256,256]{1,0:T(8,128)(2,1)S(1)}, bf16[256,256]{1,0:T(8,128)(2,1)S(1)}, f32[64,128]{1,0:T(8,128)S(1)}, f32[64,128]{1,0:T(8,128)S(1)}, f32[6...) custom-call(bf16[256,256]{1,0:T(8,128)(2,1)} %k_hbm.1, ...), custom_call_target="tpu_custom_call" | custom-call | flops 10000000 | bytes 262144 | tf_op jit(solution)/shard_map/pallas_call | solution.py:35
  1.8 3.5 %collective-permute-start = (f32[64,128]{1,0:T(8,128)S(1)}, f32[64,128]{1,0:T(8,128)S(1)}, u32[]{:S(2)}, u32[]{:S(2)}) collective-permute-start(f32[64,128]{1,0:T(8,128)S(1)} %get-tuple-element.59), channel_id=1, source_target_pairs={{0,13},{1,12},{2,15},{3,14},{4,9},{5,8},{6,11},{7,10},{8,5},{9,4},... | collective-permute-start | bytes 98312 | tf_op jit(solution)/shard_map/ppermute | solution.py:251
  5.3 0.7 %collective-permute-start.1 = (f32[64,128]{1,0:T(8,128)S(1)}, f32[64,128]{1,0:T(8,128)S(1)}, u32[]{:S(2)}, u32[]{:S(2)}) collective-permute-start(f32[64,128]{1,0:T(8,128)S(1)} %get-tuple-element.60), channel_id=1, source_target_pairs={{0,9},{1,8},{2,11},{3,10},{4,13},{5,12},{6,15},{7,14},{8,1},{9,0},... | collective-permute-start | bytes 98312 | tf_op jit(solution)/shard_map/ppermute | solution.py:251
  6.2 0.5 %collective-permute-start.8 = (f32[64,128]{1,0:T(8,128)S(1)}, f32[64,128]{1,0:T(8,128)S(1)}, u32[]{:S(2)}, u32[]{:S(2)}) collective-permute-start(f32[64,128]{1,0:T(8,128)S(1)} %get-tuple-element.67), channel_id=1, source_target_pairs={{0,1},{1,0},{2,3},{3,2},{4,5},{5,4},{6,7},{7,6},{8,9},{9,8},{10,11... | collective-permute-start | bytes 98312 | tf_op jit(solution)/shard_map/ppermute | solution.py:251
  7.1 0.5 %collective-permute-start.9 = (f32[64,128]{1,0:T(8,128)S(1)}, f32[64,128]{1,0:T(8,128)S(1)}, u32[]{:S(2)}, u32[]{:S(2)}) collective-permute-start(f32[64,128]{1,0:T(8,128)S(1)} %get-tuple-element.69), channel_id=1, source_target_pairs={{0,1},{1,0},{2,3},{3,2},{4,5},{5,4},{6,7},{7,6},{8,9},{9,8},{10,11... | collective-permute-start | bytes 98312 | tf_op jit(solution)/shard_map/ppermute | solution.py:251
  7.6 1.1 %collective-permute-done.1.refs_1_ = f32[64,128]{1,0:T(8,128)S(1)} collective-permute-done((f32[64,128]{1,0:T(8,128)S(1)}, f32[64,128]{1,0:T(8,128)S(1)}, u32[]{:S(2)}, u32[]{:S(2)}) %collective-permute-start.1) | collective-permute-done | bytes 32800 | tf_op jit(solution)/shard_map/ppermute | solution.py:251
  8.6 1.0 %collective-permute-done.2.refs_2_ = f32[64,128]{1,0:T(8,128)S(1)} collective-permute-done((f32[64,128]{1,0:T(8,128)S(1)}, f32[64,128]{1,0:T(8,128)S(1)}, u32[]{:S(2)}, u32[]{:S(2)}) %collective-permute-start.2) | collective-permute-done | bytes 32800 | tf_op jit(solution)/shard_map/ppermute | solution.py:251
  9.9 1.9 %collective-permute-start.4 = (f32[64,128]{1,0:T(8,128)S(1)}, f32[64,128]{1,0:T(8,128)S(1)}, u32[]{:S(2)}, u32[]{:S(2)}) collective-permute-start(f32[64,128]{1,0:T(8,128)S(1)} %get-tuple-element.63), channel_id=1, source_target_pairs={{0,13},{1,8},{2,15},{3,10},{4,9},{5,12},{6,11},{7,14},{8,5},{9,0},... | collective-permute-start | bytes 98312 | tf_op jit(solution)/shard_map/ppermute | solution.py:251
  11.8 0.9 %collective-permute-start.5 = (f32[64,128]{1,0:T(8,128)S(1)}, f32[64,128]{1,0:T(8,128)S(1)}, u32[]{:S(2)}, u32[]{:S(2)}) collective-permute-start(f32[64,128]{1,0:T(8,128)S(1)} %get-tuple-element.64), channel_id=1, source_target_pairs={{0,5},{1,12},{2,7},{3,14},{4,1},{5,8},{6,3},{7,10},{8,13},{9,4},{1... | collective-permute-start | bytes 98312 | tf_op jit(solution)/shard_map/ppermute | solution.py:251
  12.7 1.1 %collective-permute-start.6 = (f32[64,128]{1,0:T(8,128)S(1)}, f32[64,128]{1,0:T(8,128)S(1)}, u32[]{:S(2)}, u32[]{:S(2)}) collective-permute-start(f32[64,128]{1,0:T(8,128)S(1)} %get-tuple-element.65), channel_id=1, source_target_pairs={{0,9},{1,4},{2,11},{3,6},{4,13},{5,0},{6,15},{7,2},{8,1},{9,12},{1... | collective-permute-start | bytes 98312 | tf_op jit(solution)/shard_map/ppermute | solution.py:251
  13.8 0.7 %collective-permute-done.10.refs_4_ = f32[64,128]{1,0:T(8,128)S(1)} collective-permute-done((f32[64,128]{1,0:T(8,128)S(1)}, f32[64,128]{1,0:T(8,128)S(1)}, u32[]{:S(2)}, u32[]{:S(2)}) %collective-permute-start.10) | collective-permute-done | bytes 32800 | tf_op jit(solution)/shard_map/ppermute | solution.py:283
  15.1 1.0 %collective-permute-done.5.refs_1_ = f32[64,128]{1,0:T(8,128)S(1)} collective-permute-done((f32[64,128]{1,0:T(8,128)S(1)}, f32[64,128]{1,0:T(8,128)S(1)}, u32[]{:S(2)}, u32[]{:S(2)}) %collective-permute-start.5) | collective-permute-done | bytes 32800 | tf_op jit(solution)/shard_map/ppermute | solution.py:251
  16.7 1.5 %shard_map.85 = (bf16[2,256,256]{2,1,0:T(8,128)(2,1)S(1)}, f32[256,256]{1,0:T(8,128)S(1)}, bf16[256,256]{1,0:T(8,128)(2,1)S(1)}, bf16[256,256]{1,0:T(8,128)(2,1)...) custom-call(bf16[256,256]{1,0:T(8,128)(2,1)S(1)} %get-tuple-element.54.k, bf16[256,256]{1,0:T(8,128)(2,1)S(1)} %get-tuple-element.55.v, ...), custom_call_target="tpu_custom_call" | custom-call | flops 67108864 | bytes 525312 | tf_op jit(solution)/shard_map/pallas_call | solution.py:35
  18.6 1.6 %collective-permute-start.17 = (f32[2,256]{1,0:T(2,128)S(1)}, f32[2,256]{1,0:T(2,128)S(1)}, u32[]{:S(2)}, u32[]{:S(2)}) collective-permute-start(f32[2,256]{1,0:T(2,128)S(1)} %get-tuple-element.78.refs_0_), channel_id=1, source_target_pairs={{0,2},{1,3},{2,0},{3,1},{4,6},{5,7},{6,4},{7,5},{8,10},{9,11},{10,... | collective-permute-start | bytes 6152 | tf_op jit(solution)/shard_map/ppermute | solution.py:303
  20.2 0.6 %collective-permute-start.15 = (f32[2,256]{1,0:T(2,128)S(1)}, f32[2,256]{1,0:T(2,128)S(1)}, u32[]{:S(2)}, u32[]{:S(2)}) collective-permute-start(f32[2,256]{1,0:T(2,128)S(1)} %get-tuple-element.78.refs_0_), channel_id=1, source_target_pairs={{0,1},{1,0},{2,3},{3,2},{4,5},{5,4},{6,7},{7,6},{8,9},{9,8},{10,11... | collective-permute-start | bytes 6152 | tf_op jit(solution)/shard_map/ppermute | solution.py:303
  20.8 1.4 %collective-permute-done.17.refs_3_ = f32[2,256]{1,0:T(2,128)S(1)} collective-permute-done((f32[2,256]{1,0:T(2,128)S(1)}, f32[2,256]{1,0:T(2,128)S(1)}, u32[]{:S(2)}, u32[]{:S(2)}) %collective-permute-start.17) | collective-permute-done | bytes 2080 | tf_op jit(solution)/shard_map/ppermute | solution.py:303
  22.2 0.9 %collective-permute-done.16.refs_2_ = f32[2,256]{1,0:T(2,128)S(1)} collective-permute-done((f32[2,256]{1,0:T(2,128)S(1)}, f32[2,256]{1,0:T(2,128)S(1)}, u32[]{:S(2)}, u32[]{:S(2)}) %collective-permute-start.16) | collective-permute-done | bytes 2080 | tf_op jit(solution)/shard_map/ppermute | solution.py:303
  23.5 0.9 %collective-permute-start.18 = (f32[64,128]{1,0:T(8,128)S(1)}, f32[64,128]{1,0:T(8,128)S(1)}, u32[]{:S(2)}, u32[]{:S(2)}) collective-permute-start(f32[64,128]{1,0:T(8,128)S(1)} %get-tuple-element.88), channel_id=1, source_target_pairs={{0,13},{1,12},{2,15},{3,14},{4,9},{5,8},{6,11},{7,10},{8,5},{9,4},... | collective-permute-start | bytes 98312 | tf_op jit(solution)/shard_map/ppermute | solution.py:251
  24.4 1.2 %collective-permute-start.19 = (f32[64,128]{1,0:T(8,128)S(1)}, f32[64,128]{1,0:T(8,128)S(1)}, u32[]{:S(2)}, u32[]{:S(2)}) collective-permute-start(f32[64,128]{1,0:T(8,128)S(1)} %get-tuple-element.89), channel_id=1, source_target_pairs={{0,9},{1,8},{2,11},{3,10},{4,13},{5,12},{6,15},{7,14},{8,1},{9,0},... | collective-permute-start | bytes 98312 | tf_op jit(solution)/shard_map/ppermute | solution.py:251
  25.6 0.9 %collective-permute-start.20 = (f32[64,128]{1,0:T(8,128)S(1)}, f32[64,128]{1,0:T(8,128)S(1)}, u32[]{:S(2)}, u32[]{:S(2)}) collective-permute-start(f32[64,128]{1,0:T(8,128)S(1)} %get-tuple-element.90), channel_id=1, source_target_pairs={{0,5},{1,4},{2,7},{3,6},{4,1},{5,0},{6,3},{7,2},{8,13},{9,12},{10,... | collective-permute-start | bytes 98312 | tf_op jit(solution)/shard_map/ppermute | solution.py:251
  26.9 0.9 %collective-permute-done.18.refs_0_ = f32[64,128]{1,0:T(8,128)S(1)} collective-permute-done((f32[64,128]{1,0:T(8,128)S(1)}, f32[64,128]{1,0:T(8,128)S(1)}, u32[]{:S(2)}, u32[]{:S(2)}) %collective-permute-start.18) | collective-permute-done | bytes 32800 | tf_op jit(solution)/shard_map/ppermute | solution.py:251
  27.9 1.1 %collective-permute-done.20.refs_2_ = f32[64,128]{1,0:T(8,128)S(1)} collective-permute-done((f32[64,128]{1,0:T(8,128)S(1)}, f32[64,128]{1,0:T(8,128)S(1)}, u32[]{:S(2)}, u32[]{:S(2)}) %collective-permute-start.20) | collective-permute-done | bytes 32800 | tf_op jit(solution)/shard_map/ppermute | solution.py:251
  29.0 3.2 %collective-permute-start.22 = (f32[64,128]{1,0:T(8,128)S(1)}, f32[64,128]{1,0:T(8,128)S(1)}, u32[]{:S(2)}, u32[]{:S(2)}) collective-permute-start(f32[64,128]{1,0:T(8,128)S(1)} %get-tuple-element.93), channel_id=1, source_target_pairs={{0,16},{4,20},{8,24},{12,28},{16,0},{20,4},{24,8},{28,12},{1,17},{... | collective-permute-start | bytes 98312 | tf_op jit(solution)/shard_map/ppermute | solution.py:283
  32.2 0.5 %collective-permute-start.28 = (f32[64,128]{1,0:T(8,128)S(1)}, f32[64,128]{1,0:T(8,128)S(1)}, u32[]{:S(2)}, u32[]{:S(2)}) collective-permute-start(f32[64,128]{1,0:T(8,128)S(1)} %get-tuple-element.99), channel_id=1, source_target_pairs={{0,1},{1,0},{2,3},{3,2},{4,5},{5,4},{6,7},{7,6},{8,9},{9,8},{10,11... | collective-permute-start | bytes 98312 | tf_op jit(solution)/shard_map/ppermute | solution.py:251
  32.7 0.5 %collective-permute-start.30 = (f32[64,128]{1,0:T(8,128)S(1)}, f32[64,128]{1,0:T(8,128)S(1)}, u32[]{:S(2)}, u32[]{:S(2)}) collective-permute-start(f32[64,128]{1,0:T(8,128)S(1)} %get-tuple-element.101), channel_id=1, source_target_pairs={{0,1},{1,0},{2,3},{3,2},{4,5},{5,4},{6,7},{7,6},{8,9},{9,8},{10,11... | collective-permute-start | bytes 98312 | tf_op jit(solution)/shard_map/ppermute | solution.py:251
  33.2 1.0 %collective-permute-done.22.over = f32[64,128]{1,0:T(8,128)S(1)} collective-permute-done((f32[64,128]{1,0:T(8,128)S(1)}, f32[64,128]{1,0:T(8,128)S(1)}, u32[]{:S(2)}, u32[]{:S(2)}) %collective-permute-start.22) | collective-permute-done | bytes 32800 | tf_op jit(solution)/shard_map/ppermute | solution.py:283
  34.3 1.7 %collective-permute-start.24 = (f32[64,128]{1,0:T(8,128)S(1)}, f32[64,128]{1,0:T(8,128)S(1)}, u32[]{:S(2)}, u32[]{:S(2)}) collective-permute-start(f32[64,128]{1,0:T(8,128)S(1)} %get-tuple-element.95), channel_id=1, source_target_pairs={{0,5},{1,12},{2,7},{3,14},{4,1},{5,8},{6,3},{7,10},{8,13},{9,4},{1... | collective-permute-start | bytes 98312 | tf_op jit(solution)/shard_map/ppermute | solution.py:251
  36.0 0.7 %collective-permute-start.25 = (f32[64,128]{1,0:T(8,128)S(1)}, f32[64,128]{1,0:T(8,128)S(1)}, u32[]{:S(2)}, u32[]{:S(2)}) collective-permute-start(f32[64,128]{1,0:T(8,128)S(1)} %get-tuple-element.96), channel_id=1, source_target_pairs={{0,9},{1,4},{2,11},{3,6},{4,13},{5,0},{6,15},{7,2},{8,1},{9,12},{1... | collective-permute-start | bytes 98312 | tf_op jit(solution)/shard_map/ppermute | solution.py:251
  36.7 0.7 %collective-permute-start.26 = (f32[64,128]{1,0:T(8,128)S(1)}, f32[64,128]{1,0:T(8,128)S(1)}, u32[]{:S(2)}, u32[]{:S(2)}) collective-permute-start(f32[64,128]{1,0:T(8,128)S(1)} %get-tuple-element.97), channel_id=1, source_target_pairs={{0,1},{1,0},{2,3},{3,2},{4,5},{5,4},{6,7},{7,6},{8,9},{9,8},{10,11... | collective-permute-start | bytes 98312 | tf_op jit(solution)/shard_map/ppermute | solution.py:251
  37.4 1.4 %shard_map.90 = (bf16[256,256]{1,0:T(8,128)(2,1)}, bf16[256,256]{1,0:T(8,128)(2,1)}, f32[256,256]{1,0:T(8,128)S(1)}, f32[256,256]{1,0:T(8,128)S(1)}) custom-call(bf16[256,256]{1,0:T(8,128)(2,1)S(1)} %get-tuple-element.79.ga, bf16[256,256]{1,0:T(8,128)(2,1)S(1)} %get-tuple-element.56.q, bf16[256,256]{1,0:T(8,128)(2,1)S(1)} %get-tuple-element.54.k, ...), custom_call_target="tpu_custom_call" | custom-call | flops 150994944 | bytes 1311744 | tf_op jit(solution)/shard_map/pallas_call | solution.py:35
  38.8 0.7 %collective-permute-done.25.refs_2_ = f32[64,128]{1,0:T(8,128)S(1)} collective-permute-done((f32[64,128]{1,0:T(8,128)S(1)}, f32[64,128]{1,0:T(8,128)S(1)}, u32[]{:S(2)}, u32[]{:S(2)}) %collective-permute-start.25) | collective-permute-done | bytes 32800 | tf_op jit(solution)/shard_map/ppermute | solution.py:251
  39.5 0.9 %shard_map.93 = (bf16[256,256]{1,0:T(8,128)(2,1)}, bf16[256,256]{1,0:T(8,128)(2,1)}) custom-call(bf16[256,256]{1,0:T(8,128)(2,1)S(1)} %get-tuple-element.54.k, bf16[256,256]{1,0:T(8,128)(2,1)S(1)} %get-tuple-element.55.v, f32[256,256]{1,0:T(8,128)S(1)} %get-tuple-element.86.gk_part, f32[256,256]{1,0:T(8,128)S(1)} %get-tuple-element.87.gv_part, ...), custom_call_target="tpu_custom_call" | custom-call | flops 10000000 | bytes 1048576 | tf_op jit(solution)/shard_map/pallas_call | solution.py:35
  (40 shorter events, 3.4 us)
Async XLA Ops:
  1.8 5.2 %collective-permute-start = (f32[64,128]{1,0:T(8,128)S(1)}, f32[64,128]{1,0:T(8,128)S(1)}, u32[]{:S(2)}, u32[]{:S(2)}) collective-permute-start(f32[64,128]{1,0:T(8,128)S(1)} %get-tuple-element.59), channel_id=1, source_target_pairs={{0,13},{1,12},{2,15},{3,14},{4,9},{5,8},{6,11},{7,10},{8,5},{9,4},... | collective-permute-start | bytes 98312 | tf_op jit(solution)/shard_map/ppermute | solution.py:251
  5.3 3.3 %collective-permute-start.1 = (f32[64,128]{1,0:T(8,128)S(1)}, f32[64,128]{1,0:T(8,128)S(1)}, u32[]{:S(2)}, u32[]{:S(2)}) collective-permute-start(f32[64,128]{1,0:T(8,128)S(1)} %get-tuple-element.60), channel_id=1, source_target_pairs={{0,9},{1,8},{2,11},{3,10},{4,13},{5,12},{6,15},{7,14},{8,1},{9,0},... | collective-permute-start | bytes 98312 | tf_op jit(solution)/shard_map/ppermute | solution.py:251
  6.0 3.6 %collective-permute-start.2 = (f32[64,128]{1,0:T(8,128)S(1)}, f32[64,128]{1,0:T(8,128)S(1)}, u32[]{:S(2)}, u32[]{:S(2)}) collective-permute-start(f32[64,128]{1,0:T(8,128)S(1)} %get-tuple-element.61), channel_id=1, source_target_pairs={{0,5},{1,4},{2,7},{3,6},{4,1},{5,0},{6,3},{7,2},{8,13},{9,12},{10,... | collective-permute-start | bytes 98312 | tf_op jit(solution)/shard_map/ppermute | solution.py:251
  6.2 3.4 %collective-permute-start.3 = (f32[64,128]{1,0:T(8,128)S(1)}, f32[64,128]{1,0:T(8,128)S(1)}, u32[]{:S(2)}, u32[]{:S(2)}) collective-permute-start(f32[64,128]{1,0:T(8,128)S(1)} %get-tuple-element.62), channel_id=1, source_target_pairs={{0,1},{1,0},{2,3},{3,2},{4,5},{5,4},{6,7},{7,6},{8,9},{9,8},{10,11... | collective-permute-start | bytes 98312 | tf_op jit(solution)/shard_map/ppermute | solution.py:251
  6.2 6.5 %collective-permute-start.8 = (f32[64,128]{1,0:T(8,128)S(1)}, f32[64,128]{1,0:T(8,128)S(1)}, u32[]{:S(2)}, u32[]{:S(2)}) collective-permute-start(f32[64,128]{1,0:T(8,128)S(1)} %get-tuple-element.67), channel_id=1, source_target_pairs={{0,1},{1,0},{2,3},{3,2},{4,5},{5,4},{6,7},{7,6},{8,9},{9,8},{10,11... | collective-permute-start | bytes 98312 | tf_op jit(solution)/shard_map/ppermute | solution.py:251
  7.1 6.8 %collective-permute-start.9 = (f32[64,128]{1,0:T(8,128)S(1)}, f32[64,128]{1,0:T(8,128)S(1)}, u32[]{:S(2)}, u32[]{:S(2)}) collective-permute-start(f32[64,128]{1,0:T(8,128)S(1)} %get-tuple-element.69), channel_id=1, source_target_pairs={{0,1},{1,0},{2,3},{3,2},{4,5},{5,4},{6,7},{7,6},{8,9},{9,8},{10,11... | collective-permute-start | bytes 98312 | tf_op jit(solution)/shard_map/ppermute | solution.py:251
  9.6 4.9 %collective-permute-start.10 = (f32[64,128]{1,0:T(8,128)S(1)}, f32[64,128]{1,0:T(8,128)S(1)}, u32[]{:S(2)}, u32[]{:S(2)}) collective-permute-start(f32[64,128]{1,0:T(8,128)S(1)} %get-tuple-element.71), channel_id=1, source_target_pairs={{0,16},{4,20},{8,24},{12,28},{16,0},{20,4},{24,8},{28,12},{1,17},{... | collective-permute-start | bytes 98312 | tf_op jit(solution)/shard_map/ppermute | solution.py:283
  9.9 4.7 %collective-permute-start.4 = (f32[64,128]{1,0:T(8,128)S(1)}, f32[64,128]{1,0:T(8,128)S(1)}, u32[]{:S(2)}, u32[]{:S(2)}) collective-permute-start(f32[64,128]{1,0:T(8,128)S(1)} %get-tuple-element.63), channel_id=1, source_target_pairs={{0,13},{1,8},{2,15},{3,10},{4,9},{5,12},{6,11},{7,14},{8,5},{9,0},... | collective-permute-start | bytes 98312 | tf_op jit(solution)/shard_map/ppermute | solution.py:251
  11.8 4.3 %collective-permute-start.5 = (f32[64,128]{1,0:T(8,128)S(1)}, f32[64,128]{1,0:T(8,128)S(1)}, u32[]{:S(2)}, u32[]{:S(2)}) collective-permute-start(f32[64,128]{1,0:T(8,128)S(1)} %get-tuple-element.64), channel_id=1, source_target_pairs={{0,5},{1,12},{2,7},{3,14},{4,1},{5,8},{6,3},{7,10},{8,13},{9,4},{1... | collective-permute-start | bytes 98312 | tf_op jit(solution)/shard_map/ppermute | solution.py:251
  12.7 3.7 %collective-permute-start.6 = (f32[64,128]{1,0:T(8,128)S(1)}, f32[64,128]{1,0:T(8,128)S(1)}, u32[]{:S(2)}, u32[]{:S(2)}) collective-permute-start(f32[64,128]{1,0:T(8,128)S(1)} %get-tuple-element.65), channel_id=1, source_target_pairs={{0,9},{1,4},{2,11},{3,6},{4,13},{5,0},{6,15},{7,2},{8,1},{9,12},{1... | collective-permute-start | bytes 98312 | tf_op jit(solution)/shard_map/ppermute | solution.py:251
  13.8 4.3 %collective-permute-start.7 = (f32[64,128]{1,0:T(8,128)S(1)}, f32[64,128]{1,0:T(8,128)S(1)}, u32[]{:S(2)}, u32[]{:S(2)}) collective-permute-start(f32[64,128]{1,0:T(8,128)S(1)} %get-tuple-element.66), channel_id=1, source_target_pairs={{0,1},{1,0},{2,3},{3,2},{4,5},{5,4},{6,7},{7,6},{8,9},{9,8},{10,11... | collective-permute-start | bytes 98312 | tf_op jit(solution)/shard_map/ppermute | solution.py:251
  14.6 3.6 %collective-permute-start.11 = (f32[64,128]{1,0:T(8,128)S(1)}, f32[64,128]{1,0:T(8,128)S(1)}, u32[]{:S(2)}, u32[]{:S(2)}) collective-permute-start(f32[64,128]{1,0:T(8,128)S(1)} %get-tuple-element.72), channel_id=1, source_target_pairs={{0,1},{1,0},{2,3},{3,2},{4,5},{5,4},{6,7},{7,6},{8,9},{9,8},{10,11... | collective-permute-start | bytes 98312 | tf_op jit(solution)/shard_map/ppermute | solution.py:251
  14.6 3.6 %collective-permute-start.12 = (f32[64,128]{1,0:T(8,128)S(1)}, f32[64,128]{1,0:T(8,128)S(1)}, u32[]{:S(2)}, u32[]{:S(2)}) collective-permute-start(f32[64,128]{1,0:T(8,128)S(1)} %get-tuple-element.73), channel_id=1, source_target_pairs={{0,1},{1,0},{2,3},{3,2},{4,5},{5,4},{6,7},{7,6},{8,9},{9,8},{10,11... | collective-permute-start | bytes 98312 | tf_op jit(solution)/shard_map/ppermute | solution.py:251
  16.2 2.0 %collective-permute-start.13 = (f32[64,128]{1,0:T(8,128)S(1)}, f32[64,128]{1,0:T(8,128)S(1)}, u32[]{:S(2)}, u32[]{:S(2)}) collective-permute-start(f32[64,128]{1,0:T(8,128)S(1)} %get-tuple-element.74), channel_id=1, source_target_pairs={{0,1},{1,0},{2,3},{3,2},{4,5},{5,4},{6,7},{7,6},{8,9},{9,8},{10,11... | collective-permute-start | bytes 98312 | tf_op jit(solution)/shard_map/ppermute | solution.py:251
  16.4 1.8 %collective-permute-start.14 = (f32[64,128]{1,0:T(8,128)S(1)}, f32[64,128]{1,0:T(8,128)S(1)}, u32[]{:S(2)}, u32[]{:S(2)}) collective-permute-start(f32[64,128]{1,0:T(8,128)S(1)} %get-tuple-element.75), channel_id=1, source_target_pairs={{0,1},{1,0},{2,3},{3,2},{4,5},{5,4},{6,7},{7,6},{8,9},{9,8},{10,11... | collective-permute-start | bytes 98312 | tf_op jit(solution)/shard_map/ppermute | solution.py:251
  18.6 3.6 %collective-permute-start.17 = (f32[2,256]{1,0:T(2,128)S(1)}, f32[2,256]{1,0:T(2,128)S(1)}, u32[]{:S(2)}, u32[]{:S(2)}) collective-permute-start(f32[2,256]{1,0:T(2,128)S(1)} %get-tuple-element.78.refs_0_), channel_id=1, source_target_pairs={{0,2},{1,3},{2,0},{3,1},{4,6},{5,7},{6,4},{7,5},{8,10},{9,11},{10,... | collective-permute-start | bytes 6152 | tf_op jit(solution)/shard_map/ppermute | solution.py:303
  20.1 3.0 %collective-permute-start.16 = (f32[2,256]{1,0:T(2,128)S(1)}, f32[2,256]{1,0:T(2,128)S(1)}, u32[]{:S(2)}, u32[]{:S(2)}) collective-permute-start(f32[2,256]{1,0:T(2,128)S(1)} %get-tuple-element.78.refs_0_), channel_id=1, source_target_pairs={{0,3},{1,2},{2,1},{3,0},{4,7},{5,6},{6,5},{7,4},{8,11},{9,10},{10,... | collective-permute-start | bytes 6152 | tf_op jit(solution)/shard_map/ppermute | solution.py:303
  20.2 2.9 %collective-permute-start.15 = (f32[2,256]{1,0:T(2,128)S(1)}, f32[2,256]{1,0:T(2,128)S(1)}, u32[]{:S(2)}, u32[]{:S(2)}) collective-permute-start(f32[2,256]{1,0:T(2,128)S(1)} %get-tuple-element.78.refs_0_), channel_id=1, source_target_pairs={{0,1},{1,0},{2,3},{3,2},{4,5},{5,4},{6,7},{7,6},{8,9},{9,8},{10,11... | collective-permute-start | bytes 6152 | tf_op jit(solution)/shard_map/ppermute | solution.py:303
  23.5 4.4 %collective-permute-start.18 = (f32[64,128]{1,0:T(8,128)S(1)}, f32[64,128]{1,0:T(8,128)S(1)}, u32[]{:S(2)}, u32[]{:S(2)}) collective-permute-start(f32[64,128]{1,0:T(8,128)S(1)} %get-tuple-element.88), channel_id=1, source_target_pairs={{0,13},{1,12},{2,15},{3,14},{4,9},{5,8},{6,11},{7,10},{8,5},{9,4},... | collective-permute-start | bytes 98312 | tf_op jit(solution)/shard_map/ppermute | solution.py:251
  24.4 3.5 %collective-permute-start.19 = (f32[64,128]{1,0:T(8,128)S(1)}, f32[64,128]{1,0:T(8,128)S(1)}, u32[]{:S(2)}, u32[]{:S(2)}) collective-permute-start(f32[64,128]{1,0:T(8,128)S(1)} %get-tuple-element.89), channel_id=1, source_target_pairs={{0,9},{1,8},{2,11},{3,10},{4,13},{5,12},{6,15},{7,14},{8,1},{9,0},... | collective-permute-start | bytes 98312 | tf_op jit(solution)/shard_map/ppermute | solution.py:251
  25.6 3.4 %collective-permute-start.20 = (f32[64,128]{1,0:T(8,128)S(1)}, f32[64,128]{1,0:T(8,128)S(1)}, u32[]{:S(2)}, u32[]{:S(2)}) collective-permute-start(f32[64,128]{1,0:T(8,128)S(1)} %get-tuple-element.90), channel_id=1, source_target_pairs={{0,5},{1,4},{2,7},{3,6},{4,1},{5,0},{6,3},{7,2},{8,13},{9,12},{10,... | collective-permute-start | bytes 98312 | tf_op jit(solution)/shard_map/ppermute | solution.py:251
  26.5 2.5 %collective-permute-start.21 = (f32[64,128]{1,0:T(8,128)S(1)}, f32[64,128]{1,0:T(8,128)S(1)}, u32[]{:S(2)}, u32[]{:S(2)}) collective-permute-start(f32[64,128]{1,0:T(8,128)S(1)} %get-tuple-element.91), channel_id=1, source_target_pairs={{0,1},{1,0},{2,3},{3,2},{4,5},{5,4},{6,7},{7,6},{8,9},{9,8},{10,11... | collective-permute-start | bytes 98312 | tf_op jit(solution)/shard_map/ppermute | solution.py:251
  29.0 5.2 %collective-permute-start.22 = (f32[64,128]{1,0:T(8,128)S(1)}, f32[64,128]{1,0:T(8,128)S(1)}, u32[]{:S(2)}, u32[]{:S(2)}) collective-permute-start(f32[64,128]{1,0:T(8,128)S(1)} %get-tuple-element.93), channel_id=1, source_target_pairs={{0,16},{4,20},{8,24},{12,28},{16,0},{20,4},{24,8},{28,12},{1,17},{... | collective-permute-start | bytes 98312 | tf_op jit(solution)/shard_map/ppermute | solution.py:283
  32.2 2.1 %collective-permute-start.27 = (f32[64,128]{1,0:T(8,128)S(1)}, f32[64,128]{1,0:T(8,128)S(1)}, u32[]{:S(2)}, u32[]{:S(2)}) collective-permute-start(f32[64,128]{1,0:T(8,128)S(1)} %get-tuple-element.98), channel_id=1, source_target_pairs={{0,1},{1,0},{2,3},{3,2},{4,5},{5,4},{6,7},{7,6},{8,9},{9,8},{10,11... | collective-permute-start | bytes 98312 | tf_op jit(solution)/shard_map/ppermute | solution.py:251
  32.2 3.9 %collective-permute-start.28 = (f32[64,128]{1,0:T(8,128)S(1)}, f32[64,128]{1,0:T(8,128)S(1)}, u32[]{:S(2)}, u32[]{:S(2)}) collective-permute-start(f32[64,128]{1,0:T(8,128)S(1)} %get-tuple-element.99), channel_id=1, source_target_pairs={{0,1},{1,0},{2,3},{3,2},{4,5},{5,4},{6,7},{7,6},{8,9},{9,8},{10,11... | collective-permute-start | bytes 98312 | tf_op jit(solution)/shard_map/ppermute | solution.py:251
  32.7 4.0 %collective-permute-start.29 = (f32[64,128]{1,0:T(8,128)S(1)}, f32[64,128]{1,0:T(8,128)S(1)}, u32[]{:S(2)}, u32[]{:S(2)}) collective-permute-start(f32[64,128]{1,0:T(8,128)S(1)} %get-tuple-element.100), channel_id=1, source_target_pairs={{0,1},{1,0},{2,3},{3,2},{4,5},{5,4},{6,7},{7,6},{8,9},{9,8},{10,11... | collective-permute-start | bytes 98312 | tf_op jit(solution)/shard_map/ppermute | solution.py:251
  32.7 6.1 %collective-permute-start.30 = (f32[64,128]{1,0:T(8,128)S(1)}, f32[64,128]{1,0:T(8,128)S(1)}, u32[]{:S(2)}, u32[]{:S(2)}) collective-permute-start(f32[64,128]{1,0:T(8,128)S(1)} %get-tuple-element.101), channel_id=1, source_target_pairs={{0,1},{1,0},{2,3},{3,2},{4,5},{5,4},{6,7},{7,6},{8,9},{9,8},{10,11... | collective-permute-start | bytes 98312 | tf_op jit(solution)/shard_map/ppermute | solution.py:251
  34.2 4.6 %collective-permute-start.23 = (f32[64,128]{1,0:T(8,128)S(1)}, f32[64,128]{1,0:T(8,128)S(1)}, u32[]{:S(2)}, u32[]{:S(2)}) collective-permute-start(f32[64,128]{1,0:T(8,128)S(1)} %get-tuple-element.94), channel_id=1, source_target_pairs={{0,13},{1,8},{2,15},{3,10},{4,9},{5,12},{6,11},{7,14},{8,5},{9,0},... | collective-permute-start | bytes 98312 | tf_op jit(solution)/shard_map/ppermute | solution.py:251
  34.3 4.5 %collective-permute-start.24 = (f32[64,128]{1,0:T(8,128)S(1)}, f32[64,128]{1,0:T(8,128)S(1)}, u32[]{:S(2)}, u32[]{:S(2)}) collective-permute-start(f32[64,128]{1,0:T(8,128)S(1)} %get-tuple-element.95), channel_id=1, source_target_pairs={{0,5},{1,12},{2,7},{3,14},{4,1},{5,8},{6,3},{7,10},{8,13},{9,4},{1... | collective-permute-start | bytes 98312 | tf_op jit(solution)/shard_map/ppermute | solution.py:251
  36.0 3.5 %collective-permute-start.25 = (f32[64,128]{1,0:T(8,128)S(1)}, f32[64,128]{1,0:T(8,128)S(1)}, u32[]{:S(2)}, u32[]{:S(2)}) collective-permute-start(f32[64,128]{1,0:T(8,128)S(1)} %get-tuple-element.96), channel_id=1, source_target_pairs={{0,9},{1,4},{2,11},{3,6},{4,13},{5,0},{6,15},{7,2},{8,1},{9,12},{1... | collective-permute-start | bytes 98312 | tf_op jit(solution)/shard_map/ppermute | solution.py:251
  36.7 2.8 %collective-permute-start.26 = (f32[64,128]{1,0:T(8,128)S(1)}, f32[64,128]{1,0:T(8,128)S(1)}, u32[]{:S(2)}, u32[]{:S(2)}) collective-permute-start(f32[64,128]{1,0:T(8,128)S(1)} %get-tuple-element.97), channel_id=1, source_target_pairs={{0,1},{1,0},{2,3},{3,2},{4,5},{5,4},{6,7},{7,6},{8,9},{9,8},{10,11... | collective-permute-start | bytes 98312 | tf_op jit(solution)/shard_map/ppermute | solution.py:251

commit v2 on v1

--- a/solution.py
+++ b/solution.py
@@ -60,7 +60,7 @@
 
 def step_of(i, odd, order):
     return (
-        (3, 2, 1, 0),
+        (3, 1, 2, 0),
         (3, 2, 1, 0),
         (3 - odd, 1 + 2 * odd, 2 - odd, 0),
     )[order][i]

time: 40.7 us -> 40.8 us (level)
  waiting for transfers between devices: 10.5 us -> 11.1 us
  starting transfers between devices: 23.4 us -> 22.9 us
    ppermute x2, waiting for transfers between devices: 1.68 us -> 2.36 us  [carried_in(): over = lax.ppermute(total, 'ctx', [(j, j ^ group) for j in both])]
  transfers between devices with their start and end apart: 31 -> 31, of which waited for: 12 -> 13; matrix products, arithmetic and copies ran while one was open for 0% -> 0% of each run, Pallas kernels for 7% -> 7%
where the time goes in v2:
time: 40.8 us; the launch traced here: 40.6 us
  starting transfers between devices  22.9 us (56%)
  waiting for transfers between devices  11.1 us (27%)
  Pallas kernels  5.78 us (14%)
  between operations  0.77 us (2%)
    ppermute x26, starting transfers between devices, exchange(): return lax.ppermute(piece, ('ctx', 'tp'), pairs)  17.5 us
    ppermute x26, waiting for transfers between devices, exchange(): return lax.ppermute(piece, ('ctx', 'tp'), pairs)  6.37 us
    pallas_call x10, Pallas kernels, call(): pl.pallas_call(body, out_shape=outs, in_specs=ins or [VMEM] * len(args),...  5.78 us
    ppermute x2, starting transfers between devices, carried_in(): over = lax.ppermute(total, 'ctx', [(j, j ^ group) for j in both])  3.21 us
    ppermute x3, waiting for transfers between devices, from_all(): lax.ppermute(part, axis, [(i, i ^ step if even else (i + step) % count) f...  2.39 us
    ppermute x2, waiting for transfers between devices, carried_in(): over = lax.ppermute(total, 'ctx', [(j, j ^ group) for j in both])  2.36 us
    ppermute x3, starting transfers between devices, from_all(): lax.ppermute(part, axis, [(i, i ^ step if even else (i + step) % count) f...  2.2 us
  transfers between devices with their start and end apart: 31, of which 13 were waited for; matrix products, arithmetic and copies ran while one was open for 0% of the time, Pallas kernels for 7%

profile of v2, /device:TPU:0, one launch (start us, length us, event | category | flops | bytes accessed | tf_op | source)
XLA Modules:
  0.0 40.6 jit_solution(8818759307505007096)
XLA Ops:
  0.6 1.2 %shard_map.84 = (bf16[256,256]{1,0:T(8,128)(2,1)S(1)}, bf16[256,256]{1,0:T(8,128)(2,1)S(1)}, f32[64,128]{1,0:T(8,128)S(1)}, f32[64,128]{1,0:T(8,128)S(1)}, f32[6...) custom-call(bf16[256,256]{1,0:T(8,128)(2,1)} %k_hbm.1, ...), custom_call_target="tpu_custom_call" | custom-call | flops 10000000 | bytes 262144 | tf_op jit(solution)/shard_map/pallas_call | solution.py:35
  1.8 3.5 %collective-permute-start = (f32[64,128]{1,0:T(8,128)S(1)}, f32[64,128]{1,0:T(8,128)S(1)}, u32[]{:S(2)}, u32[]{:S(2)}) collective-permute-start(f32[64,128]{1,0:T(8,128)S(1)} %get-tuple-element.59), channel_id=1, source_target_pairs={{0,13},{1,12},{2,15},{3,14},{4,9},{5,8},{6,11},{7,10},{8,5},{9,4},... | collective-permute-start | bytes 98312 | tf_op jit(solution)/shard_map/ppermute | solution.py:251
  5.3 0.8 %collective-permute-start.1 = (f32[64,128]{1,0:T(8,128)S(1)}, f32[64,128]{1,0:T(8,128)S(1)}, u32[]{:S(2)}, u32[]{:S(2)}) collective-permute-start(f32[64,128]{1,0:T(8,128)S(1)} %get-tuple-element.60), channel_id=1, source_target_pairs={{0,5},{1,4},{2,7},{3,6},{4,1},{5,0},{6,3},{7,2},{8,13},{9,12},{10,... | collective-permute-start | bytes 98312 | tf_op jit(solution)/shard_map/ppermute | solution.py:251
  6.2 0.5 %collective-permute-start.8 = (f32[64,128]{1,0:T(8,128)S(1)}, f32[64,128]{1,0:T(8,128)S(1)}, u32[]{:S(2)}, u32[]{:S(2)}) collective-permute-start(f32[64,128]{1,0:T(8,128)S(1)} %get-tuple-element.67), channel_id=1, source_target_pairs={{0,1},{1,0},{2,3},{3,2},{4,5},{5,4},{6,7},{7,6},{8,9},{9,8},{10,11... | collective-permute-start | bytes 98312 | tf_op jit(solution)/shard_map/ppermute | solution.py:251
  7.1 0.5 %collective-permute-start.9 = (f32[64,128]{1,0:T(8,128)S(1)}, f32[64,128]{1,0:T(8,128)S(1)}, u32[]{:S(2)}, u32[]{:S(2)}) collective-permute-start(f32[64,128]{1,0:T(8,128)S(1)} %get-tuple-element.69), channel_id=1, source_target_pairs={{0,1},{1,0},{2,3},{3,2},{4,5},{5,4},{6,7},{7,6},{8,9},{9,8},{10,11... | collective-permute-start | bytes 98312 | tf_op jit(solution)/shard_map/ppermute | solution.py:251
  7.6 1.1 %collective-permute-done.1.refs_1_ = f32[64,128]{1,0:T(8,128)S(1)} collective-permute-done((f32[64,128]{1,0:T(8,128)S(1)}, f32[64,128]{1,0:T(8,128)S(1)}, u32[]{:S(2)}, u32[]{:S(2)}) %collective-permute-start.1) | collective-permute-done | bytes 32800 | tf_op jit(solution)/shard_map/ppermute | solution.py:251
  8.6 1.1 %collective-permute-done.2.refs_2_ = f32[64,128]{1,0:T(8,128)S(1)} collective-permute-done((f32[64,128]{1,0:T(8,128)S(1)}, f32[64,128]{1,0:T(8,128)S(1)}, u32[]{:S(2)}, u32[]{:S(2)}) %collective-permute-start.2) | collective-permute-done | bytes 32800 | tf_op jit(solution)/shard_map/ppermute | solution.py:251
  9.9 1.9 %collective-permute-start.4 = (f32[64,128]{1,0:T(8,128)S(1)}, f32[64,128]{1,0:T(8,128)S(1)}, u32[]{:S(2)}, u32[]{:S(2)}) collective-permute-start(f32[64,128]{1,0:T(8,128)S(1)} %get-tuple-element.63), channel_id=1, source_target_pairs={{0,13},{1,8},{2,15},{3,10},{4,9},{5,12},{6,11},{7,14},{8,5},{9,0},... | collective-permute-start | bytes 98312 | tf_op jit(solution)/shard_map/ppermute | solution.py:251
  11.8 0.9 %collective-permute-start.5 = (f32[64,128]{1,0:T(8,128)S(1)}, f32[64,128]{1,0:T(8,128)S(1)}, u32[]{:S(2)}, u32[]{:S(2)}) collective-permute-start(f32[64,128]{1,0:T(8,128)S(1)} %get-tuple-element.64), channel_id=1, source_target_pairs={{0,5},{1,12},{2,7},{3,14},{4,1},{5,8},{6,3},{7,10},{8,13},{9,4},{1... | collective-permute-start | bytes 98312 | tf_op jit(solution)/shard_map/ppermute | solution.py:251
  12.7 0.8 %collective-permute-start.6 = (f32[64,128]{1,0:T(8,128)S(1)}, f32[64,128]{1,0:T(8,128)S(1)}, u32[]{:S(2)}, u32[]{:S(2)}) collective-permute-start(f32[64,128]{1,0:T(8,128)S(1)} %get-tuple-element.65), channel_id=1, source_target_pairs={{0,9},{1,4},{2,11},{3,6},{4,13},{5,0},{6,15},{7,2},{8,1},{9,12},{1... | collective-permute-start | bytes 98312 | tf_op jit(solution)/shard_map/ppermute | solution.py:251
  13.5 1.3 %collective-permute-done.10.refs_4_ = f32[64,128]{1,0:T(8,128)S(1)} collective-permute-done((f32[64,128]{1,0:T(8,128)S(1)}, f32[64,128]{1,0:T(8,128)S(1)}, u32[]{:S(2)}, u32[]{:S(2)}) %collective-permute-start.10) | collective-permute-done | bytes 32800 | tf_op jit(solution)/shard_map/ppermute | solution.py:283
  14.9 0.5 %collective-permute-start.12 = (f32[64,128]{1,0:T(8,128)S(1)}, f32[64,128]{1,0:T(8,128)S(1)}, u32[]{:S(2)}, u32[]{:S(2)}) collective-permute-start(f32[64,128]{1,0:T(8,128)S(1)} %get-tuple-element.73), channel_id=1, source_target_pairs={{0,1},{1,0},{2,3},{3,2},{4,5},{5,4},{6,7},{7,6},{8,9},{9,8},{10,11... | collective-permute-start | bytes 98312 | tf_op jit(solution)/shard_map/ppermute | solution.py:251
  15.4 0.8 %collective-permute-done.5.refs_1_ = f32[64,128]{1,0:T(8,128)S(1)} collective-permute-done((f32[64,128]{1,0:T(8,128)S(1)}, f32[64,128]{1,0:T(8,128)S(1)}, u32[]{:S(2)}, u32[]{:S(2)}) %collective-permute-start.5) | collective-permute-done | bytes 32800 | tf_op jit(solution)/shard_map/ppermute | solution.py:251
  16.7 1.5 %shard_map.85 = (bf16[2,256,256]{2,1,0:T(8,128)(2,1)S(1)}, f32[256,256]{1,0:T(8,128)S(1)}, bf16[256,256]{1,0:T(8,128)(2,1)S(1)}, bf16[256,256]{1,0:T(8,128)(2,1)...) custom-call(bf16[256,256]{1,0:T(8,128)(2,1)S(1)} %get-tuple-element.54.k, bf16[256,256]{1,0:T(8,128)(2,1)S(1)} %get-tuple-element.55.v, ...), custom_call_target="tpu_custom_call" | custom-call | flops 67108864 | bytes 525312 | tf_op jit(solution)/shard_map/pallas_call | solution.py:35
  18.6 1.6 %collective-permute-start.17 = (f32[2,256]{1,0:T(2,128)S(1)}, f32[2,256]{1,0:T(2,128)S(1)}, u32[]{:S(2)}, u32[]{:S(2)}) collective-permute-start(f32[2,256]{1,0:T(2,128)S(1)} %get-tuple-element.78.refs_0_), channel_id=1, source_target_pairs={{0,2},{1,3},{2,0},{3,1},{4,6},{5,7},{6,4},{7,5},{8,10},{9,11},{10,... | collective-permute-start | bytes 6152 | tf_op jit(solution)/shard_map/ppermute | solution.py:303
  20.2 0.6 %collective-permute-start.15 = (f32[2,256]{1,0:T(2,128)S(1)}, f32[2,256]{1,0:T(2,128)S(1)}, u32[]{:S(2)}, u32[]{:S(2)}) collective-permute-start(f32[2,256]{1,0:T(2,128)S(1)} %get-tuple-element.78.refs_0_), channel_id=1, source_target_pairs={{0,1},{1,0},{2,3},{3,2},{4,5},{5,4},{6,7},{7,6},{8,9},{9,8},{10,11... | collective-permute-start | bytes 6152 | tf_op jit(solution)/shard_map/ppermute | solution.py:303
  20.8 1.4 %collective-permute-done.17.refs_3_ = f32[2,256]{1,0:T(2,128)S(1)} collective-permute-done((f32[2,256]{1,0:T(2,128)S(1)}, f32[2,256]{1,0:T(2,128)S(1)}, u32[]{:S(2)}, u32[]{:S(2)}) %collective-permute-start.17) | collective-permute-done | bytes 2080 | tf_op jit(solution)/shard_map/ppermute | solution.py:303
  22.3 0.9 %collective-permute-done.16.refs_2_ = f32[2,256]{1,0:T(2,128)S(1)} collective-permute-done((f32[2,256]{1,0:T(2,128)S(1)}, f32[2,256]{1,0:T(2,128)S(1)}, u32[]{:S(2)}, u32[]{:S(2)}) %collective-permute-start.16) | collective-permute-done | bytes 2080 | tf_op jit(solution)/shard_map/ppermute | solution.py:303
  23.5 0.9 %collective-permute-start.18 = (f32[64,128]{1,0:T(8,128)S(1)}, f32[64,128]{1,0:T(8,128)S(1)}, u32[]{:S(2)}, u32[]{:S(2)}) collective-permute-start(f32[64,128]{1,0:T(8,128)S(1)} %get-tuple-element.88), channel_id=1, source_target_pairs={{0,13},{1,12},{2,15},{3,14},{4,9},{5,8},{6,11},{7,10},{8,5},{9,4},... | collective-permute-start | bytes 98312 | tf_op jit(solution)/shard_map/ppermute | solution.py:251
  24.4 1.2 %collective-permute-start.19 = (f32[64,128]{1,0:T(8,128)S(1)}, f32[64,128]{1,0:T(8,128)S(1)}, u32[]{:S(2)}, u32[]{:S(2)}) collective-permute-start(f32[64,128]{1,0:T(8,128)S(1)} %get-tuple-element.89), channel_id=1, source_target_pairs={{0,9},{1,8},{2,11},{3,10},{4,13},{5,12},{6,15},{7,14},{8,1},{9,0},... | collective-permute-start | bytes 98312 | tf_op jit(solution)/shard_map/ppermute | solution.py:251
  25.7 0.9 %collective-permute-start.20 = (f32[64,128]{1,0:T(8,128)S(1)}, f32[64,128]{1,0:T(8,128)S(1)}, u32[]{:S(2)}, u32[]{:S(2)}) collective-permute-start(f32[64,128]{1,0:T(8,128)S(1)} %get-tuple-element.90), channel_id=1, source_target_pairs={{0,5},{1,4},{2,7},{3,6},{4,1},{5,0},{6,3},{7,2},{8,13},{9,12},{10,... | collective-permute-start | bytes 98312 | tf_op jit(solution)/shard_map/ppermute | solution.py:251
  26.9 1.0 %collective-permute-done.18.refs_0_ = f32[64,128]{1,0:T(8,128)S(1)} collective-permute-done((f32[64,128]{1,0:T(8,128)S(1)}, f32[64,128]{1,0:T(8,128)S(1)}, u32[]{:S(2)}, u32[]{:S(2)}) %collective-permute-start.18) | collective-permute-done | bytes 32800 | tf_op jit(solution)/shard_map/ppermute | solution.py:251
  28.0 1.1 %collective-permute-done.20.refs_2_ = f32[64,128]{1,0:T(8,128)S(1)} collective-permute-done((f32[64,128]{1,0:T(8,128)S(1)}, f32[64,128]{1,0:T(8,128)S(1)}, u32[]{:S(2)}, u32[]{:S(2)}) %collective-permute-start.20) | collective-permute-done | bytes 32800 | tf_op jit(solution)/shard_map/ppermute | solution.py:251
  29.1 3.1 %collective-permute-start.22 = (f32[64,128]{1,0:T(8,128)S(1)}, f32[64,128]{1,0:T(8,128)S(1)}, u32[]{:S(2)}, u32[]{:S(2)}) collective-permute-start(f32[64,128]{1,0:T(8,128)S(1)} %get-tuple-element.93), channel_id=1, source_target_pairs={{0,16},{4,20},{8,24},{12,28},{16,0},{20,4},{24,8},{28,12},{1,17},{... | collective-permute-start | bytes 98312 | tf_op jit(solution)/shard_map/ppermute | solution.py:283
  32.2 0.5 %collective-permute-start.28 = (f32[64,128]{1,0:T(8,128)S(1)}, f32[64,128]{1,0:T(8,128)S(1)}, u32[]{:S(2)}, u32[]{:S(2)}) collective-permute-start(f32[64,128]{1,0:T(8,128)S(1)} %get-tuple-element.99), channel_id=1, source_target_pairs={{0,1},{1,0},{2,3},{3,2},{4,5},{5,4},{6,7},{7,6},{8,9},{9,8},{10,11... | collective-permute-start | bytes 98312 | tf_op jit(solution)/shard_map/ppermute | solution.py:251
  32.7 0.5 %collective-permute-start.30 = (f32[64,128]{1,0:T(8,128)S(1)}, f32[64,128]{1,0:T(8,128)S(1)}, u32[]{:S(2)}, u32[]{:S(2)}) collective-permute-start(f32[64,128]{1,0:T(8,128)S(1)} %get-tuple-element.101), channel_id=1, source_target_pairs={{0,1},{1,0},{2,3},{3,2},{4,5},{5,4},{6,7},{7,6},{8,9},{9,8},{10,11... | collective-permute-start | bytes 98312 | tf_op jit(solution)/shard_map/ppermute | solution.py:251
  33.2 1.1 %collective-permute-done.22.over = f32[64,128]{1,0:T(8,128)S(1)} collective-permute-done((f32[64,128]{1,0:T(8,128)S(1)}, f32[64,128]{1,0:T(8,128)S(1)}, u32[]{:S(2)}, u32[]{:S(2)}) %collective-permute-start.22) | collective-permute-done | bytes 32800 | tf_op jit(solution)/shard_map/ppermute | solution.py:283
  34.4 1.7 %collective-permute-start.24 = (f32[64,128]{1,0:T(8,128)S(1)}, f32[64,128]{1,0:T(8,128)S(1)}, u32[]{:S(2)}, u32[]{:S(2)}) collective-permute-start(f32[64,128]{1,0:T(8,128)S(1)} %get-tuple-element.95), channel_id=1, source_target_pairs={{0,5},{1,12},{2,7},{3,14},{4,1},{5,8},{6,3},{7,10},{8,13},{9,4},{1... | collective-permute-start | bytes 98312 | tf_op jit(solution)/shard_map/ppermute | solution.py:251
  36.0 1.0 %collective-permute-start.25 = (f32[64,128]{1,0:T(8,128)S(1)}, f32[64,128]{1,0:T(8,128)S(1)}, u32[]{:S(2)}, u32[]{:S(2)}) collective-permute-start(f32[64,128]{1,0:T(8,128)S(1)} %get-tuple-element.96), channel_id=1, source_target_pairs={{0,9},{1,4},{2,11},{3,6},{4,13},{5,0},{6,15},{7,2},{8,1},{9,12},{1... | collective-permute-start | bytes 98312 | tf_op jit(solution)/shard_map/ppermute | solution.py:251
  37.5 1.4 %shard_map.90 = (bf16[256,256]{1,0:T(8,128)(2,1)}, bf16[256,256]{1,0:T(8,128)(2,1)}, f32[256,256]{1,0:T(8,128)S(1)}, f32[256,256]{1,0:T(8,128)S(1)}) custom-call(bf16[256,256]{1,0:T(8,128)(2,1)S(1)} %get-tuple-element.79.ga, bf16[256,256]{1,0:T(8,128)(2,1)S(1)} %get-tuple-element.56.q, bf16[256,256]{1,0:T(8,128)(2,1)S(1)} %get-tuple-element.54.k, ...), custom_call_target="tpu_custom_call" | custom-call | flops 150994944 | bytes 1311744 | tf_op jit(solution)/shard_map/pallas_call | solution.py:35
  38.9 0.7 %collective-permute-done.25.refs_2_ = f32[64,128]{1,0:T(8,128)S(1)} collective-permute-done((f32[64,128]{1,0:T(8,128)S(1)}, f32[64,128]{1,0:T(8,128)S(1)}, u32[]{:S(2)}, u32[]{:S(2)}) %collective-permute-start.25) | collective-permute-done | bytes 32800 | tf_op jit(solution)/shard_map/ppermute | solution.py:251
  39.6 0.9 %shard_map.93 = (bf16[256,256]{1,0:T(8,128)(2,1)}, bf16[256,256]{1,0:T(8,128)(2,1)}) custom-call(bf16[256,256]{1,0:T(8,128)(2,1)S(1)} %get-tuple-element.54.k, bf16[256,256]{1,0:T(8,128)(2,1)S(1)} %get-tuple-element.55.v, f32[256,256]{1,0:T(8,128)S(1)} %get-tuple-element.86.gk_part, f32[256,256]{1,0:T(8,128)S(1)} %get-tuple-element.87.gv_part, ...), custom_call_target="tpu_custom_call" | custom-call | flops 10000000 | bytes 1048576 | tf_op jit(solution)/shard_map/pallas_call | solution.py:35
  (40 shorter events, 3.0 us)
Async XLA Ops:
  1.8 5.2 %collective-permute-start = (f32[64,128]{1,0:T(8,128)S(1)}, f32[64,128]{1,0:T(8,128)S(1)}, u32[]{:S(2)}, u32[]{:S(2)}) collective-permute-start(f32[64,128]{1,0:T(8,128)S(1)} %get-tuple-element.59), channel_id=1, source_target_pairs={{0,13},{1,12},{2,15},{3,14},{4,9},{5,8},{6,11},{7,10},{8,5},{9,4},... | collective-permute-start | bytes 98312 | tf_op jit(solution)/shard_map/ppermute | solution.py:251
  5.3 3.3 %collective-permute-start.1 = (f32[64,128]{1,0:T(8,128)S(1)}, f32[64,128]{1,0:T(8,128)S(1)}, u32[]{:S(2)}, u32[]{:S(2)}) collective-permute-start(f32[64,128]{1,0:T(8,128)S(1)} %get-tuple-element.60), channel_id=1, source_target_pairs={{0,5},{1,4},{2,7},{3,6},{4,1},{5,0},{6,3},{7,2},{8,13},{9,12},{10,... | collective-permute-start | bytes 98312 | tf_op jit(solution)/shard_map/ppermute | solution.py:251
  6.1 3.6 %collective-permute-start.2 = (f32[64,128]{1,0:T(8,128)S(1)}, f32[64,128]{1,0:T(8,128)S(1)}, u32[]{:S(2)}, u32[]{:S(2)}) collective-permute-start(f32[64,128]{1,0:T(8,128)S(1)} %get-tuple-element.61), channel_id=1, source_target_pairs={{0,9},{1,8},{2,11},{3,10},{4,13},{5,12},{6,15},{7,14},{8,1},{9,0},... | collective-permute-start | bytes 98312 | tf_op jit(solution)/shard_map/ppermute | solution.py:251
  6.2 3.5 %collective-permute-start.3 = (f32[64,128]{1,0:T(8,128)S(1)}, f32[64,128]{1,0:T(8,128)S(1)}, u32[]{:S(2)}, u32[]{:S(2)}) collective-permute-start(f32[64,128]{1,0:T(8,128)S(1)} %get-tuple-element.62), channel_id=1, source_target_pairs={{0,1},{1,0},{2,3},{3,2},{4,5},{5,4},{6,7},{7,6},{8,9},{9,8},{10,11... | collective-permute-start | bytes 98312 | tf_op jit(solution)/shard_map/ppermute | solution.py:251
  6.2 6.5 %collective-permute-start.8 = (f32[64,128]{1,0:T(8,128)S(1)}, f32[64,128]{1,0:T(8,128)S(1)}, u32[]{:S(2)}, u32[]{:S(2)}) collective-permute-start(f32[64,128]{1,0:T(8,128)S(1)} %get-tuple-element.67), channel_id=1, source_target_pairs={{0,1},{1,0},{2,3},{3,2},{4,5},{5,4},{6,7},{7,6},{8,9},{9,8},{10,11... | collective-permute-start | bytes 98312 | tf_op jit(solution)/shard_map/ppermute | solution.py:251
  7.1 6.5 %collective-permute-start.9 = (f32[64,128]{1,0:T(8,128)S(1)}, f32[64,128]{1,0:T(8,128)S(1)}, u32[]{:S(2)}, u32[]{:S(2)}) collective-permute-start(f32[64,128]{1,0:T(8,128)S(1)} %get-tuple-element.69), channel_id=1, source_target_pairs={{0,1},{1,0},{2,3},{3,2},{4,5},{5,4},{6,7},{7,6},{8,9},{9,8},{10,11... | collective-permute-start | bytes 98312 | tf_op jit(solution)/shard_map/ppermute | solution.py:251
  9.8 5.0 %collective-permute-start.10 = (f32[64,128]{1,0:T(8,128)S(1)}, f32[64,128]{1,0:T(8,128)S(1)}, u32[]{:S(2)}, u32[]{:S(2)}) collective-permute-start(f32[64,128]{1,0:T(8,128)S(1)} %get-tuple-element.71), channel_id=1, source_target_pairs={{0,16},{4,20},{8,24},{12,28},{16,0},{20,4},{24,8},{28,12},{1,17},{... | collective-permute-start | bytes 98312 | tf_op jit(solution)/shard_map/ppermute | solution.py:283
  9.9 5.0 %collective-permute-start.4 = (f32[64,128]{1,0:T(8,128)S(1)}, f32[64,128]{1,0:T(8,128)S(1)}, u32[]{:S(2)}, u32[]{:S(2)}) collective-permute-start(f32[64,128]{1,0:T(8,128)S(1)} %get-tuple-element.63), channel_id=1, source_target_pairs={{0,13},{1,8},{2,15},{3,10},{4,9},{5,12},{6,11},{7,14},{8,5},{9,0},... | collective-permute-start | bytes 98312 | tf_op jit(solution)/shard_map/ppermute | solution.py:251
  11.8 4.4 %collective-permute-start.5 = (f32[64,128]{1,0:T(8,128)S(1)}, f32[64,128]{1,0:T(8,128)S(1)}, u32[]{:S(2)}, u32[]{:S(2)}) collective-permute-start(f32[64,128]{1,0:T(8,128)S(1)} %get-tuple-element.64), channel_id=1, source_target_pairs={{0,5},{1,12},{2,7},{3,14},{4,1},{5,8},{6,3},{7,10},{8,13},{9,4},{1... | collective-permute-start | bytes 98312 | tf_op jit(solution)/shard_map/ppermute | solution.py:251
  12.7 3.7 %collective-permute-start.6 = (f32[64,128]{1,0:T(8,128)S(1)}, f32[64,128]{1,0:T(8,128)S(1)}, u32[]{:S(2)}, u32[]{:S(2)}) collective-permute-start(f32[64,128]{1,0:T(8,128)S(1)} %get-tuple-element.65), channel_id=1, source_target_pairs={{0,9},{1,4},{2,11},{3,6},{4,13},{5,0},{6,15},{7,2},{8,1},{9,12},{1... | collective-permute-start | bytes 98312 | tf_op jit(solution)/shard_map/ppermute | solution.py:251
  13.5 4.7 %collective-permute-start.7 = (f32[64,128]{1,0:T(8,128)S(1)}, f32[64,128]{1,0:T(8,128)S(1)}, u32[]{:S(2)}, u32[]{:S(2)}) collective-permute-start(f32[64,128]{1,0:T(8,128)S(1)} %get-tuple-element.66), channel_id=1, source_target_pairs={{0,1},{1,0},{2,3},{3,2},{4,5},{5,4},{6,7},{7,6},{8,9},{9,8},{10,11... | collective-permute-start | bytes 98312 | tf_op jit(solution)/shard_map/ppermute | solution.py:251
  14.9 3.4 %collective-permute-start.11 = (f32[64,128]{1,0:T(8,128)S(1)}, f32[64,128]{1,0:T(8,128)S(1)}, u32[]{:S(2)}, u32[]{:S(2)}) collective-permute-start(f32[64,128]{1,0:T(8,128)S(1)} %get-tuple-element.72), channel_id=1, source_target_pairs={{0,1},{1,0},{2,3},{3,2},{4,5},{5,4},{6,7},{7,6},{8,9},{9,8},{10,11... | collective-permute-start | bytes 98312 | tf_op jit(solution)/shard_map/ppermute | solution.py:251
  14.9 3.3 %collective-permute-start.12 = (f32[64,128]{1,0:T(8,128)S(1)}, f32[64,128]{1,0:T(8,128)S(1)}, u32[]{:S(2)}, u32[]{:S(2)}) collective-permute-start(f32[64,128]{1,0:T(8,128)S(1)} %get-tuple-element.73), channel_id=1, source_target_pairs={{0,1},{1,0},{2,3},{3,2},{4,5},{5,4},{6,7},{7,6},{8,9},{9,8},{10,11... | collective-permute-start | bytes 98312 | tf_op jit(solution)/shard_map/ppermute | solution.py:251
  16.2 2.0 %collective-permute-start.13 = (f32[64,128]{1,0:T(8,128)S(1)}, f32[64,128]{1,0:T(8,128)S(1)}, u32[]{:S(2)}, u32[]{:S(2)}) collective-permute-start(f32[64,128]{1,0:T(8,128)S(1)} %get-tuple-element.74), channel_id=1, source_target_pairs={{0,1},{1,0},{2,3},{3,2},{4,5},{5,4},{6,7},{7,6},{8,9},{9,8},{10,11... | collective-permute-start | bytes 98312 | tf_op jit(solution)/shard_map/ppermute | solution.py:251
  16.4 1.9 %collective-permute-start.14 = (f32[64,128]{1,0:T(8,128)S(1)}, f32[64,128]{1,0:T(8,128)S(1)}, u32[]{:S(2)}, u32[]{:S(2)}) collective-permute-start(f32[64,128]{1,0:T(8,128)S(1)} %get-tuple-element.75), channel_id=1, source_target_pairs={{0,1},{1,0},{2,3},{3,2},{4,5},{5,4},{6,7},{7,6},{8,9},{9,8},{10,11... | collective-permute-start | bytes 98312 | tf_op jit(solution)/shard_map/ppermute | solution.py:251
  18.6 3.6 %collective-permute-start.17 = (f32[2,256]{1,0:T(2,128)S(1)}, f32[2,256]{1,0:T(2,128)S(1)}, u32[]{:S(2)}, u32[]{:S(2)}) collective-permute-start(f32[2,256]{1,0:T(2,128)S(1)} %get-tuple-element.78.refs_0_), channel_id=1, source_target_pairs={{0,2},{1,3},{2,0},{3,1},{4,6},{5,7},{6,4},{7,5},{8,10},{9,11},{10,... | collective-permute-start | bytes 6152 | tf_op jit(solution)/shard_map/ppermute | solution.py:303
  20.2 3.0 %collective-permute-start.16 = (f32[2,256]{1,0:T(2,128)S(1)}, f32[2,256]{1,0:T(2,128)S(1)}, u32[]{:S(2)}, u32[]{:S(2)}) collective-permute-start(f32[2,256]{1,0:T(2,128)S(1)} %get-tuple-element.78.refs_0_), channel_id=1, source_target_pairs={{0,3},{1,2},{2,1},{3,0},{4,7},{5,6},{6,5},{7,4},{8,11},{9,10},{10,... | collective-permute-start | bytes 6152 | tf_op jit(solution)/shard_map/ppermute | solution.py:303
  20.2 3.0 %collective-permute-start.15 = (f32[2,256]{1,0:T(2,128)S(1)}, f32[2,256]{1,0:T(2,128)S(1)}, u32[]{:S(2)}, u32[]{:S(2)}) collective-permute-start(f32[2,256]{1,0:T(2,128)S(1)} %get-tuple-element.78.refs_0_), channel_id=1, source_target_pairs={{0,1},{1,0},{2,3},{3,2},{4,5},{5,4},{6,7},{7,6},{8,9},{9,8},{10,11... | collective-permute-start | bytes 6152 | tf_op jit(solution)/shard_map/ppermute | solution.py:303
  23.5 4.4 %collective-permute-start.18 = (f32[64,128]{1,0:T(8,128)S(1)}, f32[64,128]{1,0:T(8,128)S(1)}, u32[]{:S(2)}, u32[]{:S(2)}) collective-permute-start(f32[64,128]{1,0:T(8,128)S(1)} %get-tuple-element.88), channel_id=1, source_target_pairs={{0,13},{1,12},{2,15},{3,14},{4,9},{5,8},{6,11},{7,10},{8,5},{9,4},... | collective-permute-start | bytes 98312 | tf_op jit(solution)/shard_map/ppermute | solution.py:251
  24.4 3.5 %collective-permute-start.19 = (f32[64,128]{1,0:T(8,128)S(1)}, f32[64,128]{1,0:T(8,128)S(1)}, u32[]{:S(2)}, u32[]{:S(2)}) collective-permute-start(f32[64,128]{1,0:T(8,128)S(1)} %get-tuple-element.89), channel_id=1, source_target_pairs={{0,9},{1,8},{2,11},{3,10},{4,13},{5,12},{6,15},{7,14},{8,1},{9,0},... | collective-permute-start | bytes 98312 | tf_op jit(solution)/shard_map/ppermute | solution.py:251
  25.7 3.4 %collective-permute-start.20 = (f32[64,128]{1,0:T(8,128)S(1)}, f32[64,128]{1,0:T(8,128)S(1)}, u32[]{:S(2)}, u32[]{:S(2)}) collective-permute-start(f32[64,128]{1,0:T(8,128)S(1)} %get-tuple-element.90), channel_id=1, source_target_pairs={{0,5},{1,4},{2,7},{3,6},{4,1},{5,0},{6,3},{7,2},{8,13},{9,12},{10,... | collective-permute-start | bytes 98312 | tf_op jit(solution)/shard_map/ppermute | solution.py:251
  26.6 2.4 %collective-permute-start.21 = (f32[64,128]{1,0:T(8,128)S(1)}, f32[64,128]{1,0:T(8,128)S(1)}, u32[]{:S(2)}, u32[]{:S(2)}) collective-permute-start(f32[64,128]{1,0:T(8,128)S(1)} %get-tuple-element.91), channel_id=1, source_target_pairs={{0,1},{1,0},{2,3},{3,2},{4,5},{5,4},{6,7},{7,6},{8,9},{9,8},{10,11... | collective-permute-start | bytes 98312 | tf_op jit(solution)/shard_map/ppermute | solution.py:251
  29.1 5.2 %collective-permute-start.22 = (f32[64,128]{1,0:T(8,128)S(1)}, f32[64,128]{1,0:T(8,128)S(1)}, u32[]{:S(2)}, u32[]{:S(2)}) collective-permute-start(f32[64,128]{1,0:T(8,128)S(1)} %get-tuple-element.93), channel_id=1, source_target_pairs={{0,16},{4,20},{8,24},{12,28},{16,0},{20,4},{24,8},{28,12},{1,17},{... | collective-permute-start | bytes 98312 | tf_op jit(solution)/shard_map/ppermute | solution.py:283
  32.2 2.2 %collective-permute-start.27 = (f32[64,128]{1,0:T(8,128)S(1)}, f32[64,128]{1,0:T(8,128)S(1)}, u32[]{:S(2)}, u32[]{:S(2)}) collective-permute-start(f32[64,128]{1,0:T(8,128)S(1)} %get-tuple-element.98), channel_id=1, source_target_pairs={{0,1},{1,0},{2,3},{3,2},{4,5},{5,4},{6,7},{7,6},{8,9},{9,8},{10,11... | collective-permute-start | bytes 98312 | tf_op jit(solution)/shard_map/ppermute | solution.py:251
  32.2 3.9 %collective-permute-start.28 = (f32[64,128]{1,0:T(8,128)S(1)}, f32[64,128]{1,0:T(8,128)S(1)}, u32[]{:S(2)}, u32[]{:S(2)}) collective-permute-start(f32[64,128]{1,0:T(8,128)S(1)} %get-tuple-element.99), channel_id=1, source_target_pairs={{0,1},{1,0},{2,3},{3,2},{4,5},{5,4},{6,7},{7,6},{8,9},{9,8},{10,11... | collective-permute-start | bytes 98312 | tf_op jit(solution)/shard_map/ppermute | solution.py:251
  32.7 4.3 %collective-permute-start.29 = (f32[64,128]{1,0:T(8,128)S(1)}, f32[64,128]{1,0:T(8,128)S(1)}, u32[]{:S(2)}, u32[]{:S(2)}) collective-permute-start(f32[64,128]{1,0:T(8,128)S(1)} %get-tuple-element.100), channel_id=1, source_target_pairs={{0,1},{1,0},{2,3},{3,2},{4,5},{5,4},{6,7},{7,6},{8,9},{9,8},{10,11... | collective-permute-start | bytes 98312 | tf_op jit(solution)/shard_map/ppermute | solution.py:251
  32.7 6.2 %collective-permute-start.30 = (f32[64,128]{1,0:T(8,128)S(1)}, f32[64,128]{1,0:T(8,128)S(1)}, u32[]{:S(2)}, u32[]{:S(2)}) collective-permute-start(f32[64,128]{1,0:T(8,128)S(1)} %get-tuple-element.101), channel_id=1, source_target_pairs={{0,1},{1,0},{2,3},{3,2},{4,5},{5,4},{6,7},{7,6},{8,9},{9,8},{10,11... | collective-permute-start | bytes 98312 | tf_op jit(solution)/shard_map/ppermute | solution.py:251
  34.3 4.6 %collective-permute-start.23 = (f32[64,128]{1,0:T(8,128)S(1)}, f32[64,128]{1,0:T(8,128)S(1)}, u32[]{:S(2)}, u32[]{:S(2)}) collective-permute-start(f32[64,128]{1,0:T(8,128)S(1)} %get-tuple-element.94), channel_id=1, source_target_pairs={{0,13},{1,8},{2,15},{3,10},{4,9},{5,12},{6,11},{7,14},{8,5},{9,0},... | collective-permute-start | bytes 98312 | tf_op jit(solution)/shard_map/ppermute | solution.py:251
  34.4 4.5 %collective-permute-start.24 = (f32[64,128]{1,0:T(8,128)S(1)}, f32[64,128]{1,0:T(8,128)S(1)}, u32[]{:S(2)}, u32[]{:S(2)}) collective-permute-start(f32[64,128]{1,0:T(8,128)S(1)} %get-tuple-element.95), channel_id=1, source_target_pairs={{0,5},{1,12},{2,7},{3,14},{4,1},{5,8},{6,3},{7,10},{8,13},{9,4},{1... | collective-permute-start | bytes 98312 | tf_op jit(solution)/shard_map/ppermute | solution.py:251
  36.0 3.6 %collective-permute-start.25 = (f32[64,128]{1,0:T(8,128)S(1)}, f32[64,128]{1,0:T(8,128)S(1)}, u32[]{:S(2)}, u32[]{:S(2)}) collective-permute-start(f32[64,128]{1,0:T(8,128)S(1)} %get-tuple-element.96), channel_id=1, source_target_pairs={{0,9},{1,4},{2,11},{3,6},{4,13},{5,0},{6,15},{7,2},{8,1},{9,12},{1... | collective-permute-start | bytes 98312 | tf_op jit(solution)/shard_map/ppermute | solution.py:251
  37.0 2.6 %collective-permute-start.26 = (f32[64,128]{1,0:T(8,128)S(1)}, f32[64,128]{1,0:T(8,128)S(1)}, u32[]{:S(2)}, u32[]{:S(2)}) collective-permute-start(f32[64,128]{1,0:T(8,128)S(1)} %get-tuple-element.97), channel_id=1, source_target_pairs={{0,1},{1,0},{2,3},{3,2},{4,5},{5,4},{6,7},{7,6},{8,9},{9,8},{10,11... | collective-permute-start | bytes 98312 | tf_op jit(solution)/shard_map/ppermute | solution.py:251
